TPU v7x, 32 devices: a whole 2x2x4 slice. The times are simulated.
32 devices in a mesh: dp: 8 (over y, x, core), space: 4 (over z).
Axes of the slice: x: 2, y: 2, z: 4, core: 2. Of those that a mesh axis runs over, the one named last changes fastest.
Arguments:
- features: bfloat16 [8, 12288, 128], P('dp', 'space'), may hold values from -6 to 6
- neighbours: int32 [8, 27, 12288], P('dp', None, 'space'), may hold values from -1 to 12287, as said below
- weight: bfloat16 [27, 128, 128], replicated, may hold values from -0.109375 to 0.109375
- grad_out: bfloat16 [8, 12288, 128], P('dp', 'space'), may hold values from -6 to 6
Outputs:
- conv_out: bfloat16 [8, 12288, 128], P('dp', 'space')
- grad_in: bfloat16 [8, 12288, 128], P('dp', 'space')
- grad_w: float32 [27, 128, 128], replicated
Inputs may be any that keep to these rules, and one draw needn't show every extreme that they name: Voxels of a scene are ordered by layer, 1024 per layer and layer z holding indices z * 1024 to (z + 1) * 1024 - 1; within a layer they are ordered by cell y * 64 + x, and every grid row y of every layer holds exactly 16 active voxels, so row y of layer z holds indices z * 1024 + y * 16 onward. An entry for offset (dz, dy, dx) of a voxel in layer z, row y points into layer z + dz, row y + dy. The map is symmetric: neighbours[26 - k, neighbours[k, i]] = i wherever neighbours[k, i] >= 0, and neighbours[13, i] = i.
All inputs are finite; a program needn't handle non-finite values.
Results may differ from a plain program's by a relative error of at most 0.0055.
Values may be sent and summed in bfloat16 or wider, within the bound.
No kernel may reach another device: no remote copies, remote signals or barrier semaphores. Data moves between devices by JAX's collectives and lax.ppermute only.
A program may use at most 64 MiB of HBM per device.

v0:
```python
import functools
import math

import jax
import jax.numpy as jnp
from jax import lax
from jax.experimental import pallas as pl
from jax.experimental.pallas import tpu as pltpu
from jax.sharding import PartitionSpec as P

PSIDE = 64
ROW = PSIDE // 4
LAYER = PSIDE * ROW
T = 128
CHUNK_W = 256
CHUNK_C = 256
VMEM_LIMIT = 28 * 1024 * 1024
FULL_VMEM_LIMIT = 58 * 1024 * 1024
VMEM = pl.BlockSpec(memory_space=pltpu.VMEM)
HBM = pl.BlockSpec(memory_space=pltpu.HBM)


def offset_of(k):
    return k // 9 - 1, (k // 3) % 3 - 1, k % 3 - 1


def row_in_scene_window(neighbours, shift):
    return jnp.where(neighbours >= 0, (neighbours - shift) & (T - 1), -1)


def one_hot(hit):
    return jnp.where(hit, jnp.ones((), jnp.bfloat16), jnp.zeros((), jnp.bfloat16))


def own_side():
    return lax.bitwise_and(lax.axis_index("dp"), 1).astype(jnp.int32)


def fill_edges(xe):
    edge = jnp.zeros((ROW, xe.shape[1]), jnp.bfloat16)
    xe[0:ROW, :] = edge
    xe[xe.shape[0] - ROW :, :] = edge


def one_hot_columns(rel, k, tile):
    spot = lax.broadcasted_iota(jnp.int32, (T, T), 0).astype(jnp.bfloat16)
    row = jnp.broadcast_to(rel[k, tile : tile + 1, :], (ROW, T)).astype(jnp.bfloat16)
    return one_hot(jnp.concatenate([row] * (T // ROW), axis=0) == spot)


def gather_columns(tiles, ks, xe, origin, rel, first_tile, to_f, to_g):
    channels = xe.shape[1] // 2
    none = jnp.zeros((T, T), jnp.bfloat16)
    kept = []

    def put(k, cols, part):
        to_f[k * T : (k + 1) * T, cols] = part[:channels]
        to_g[k * T : (k + 1) * T, cols] = part[channels:]

    def put_dot(source, right, places):
        picked = jnp.dot(source, right, preferred_element_type=jnp.float32).astype(jnp.bfloat16)
        for q, (k, cols) in enumerate(places):
            put(k, cols, picked[:, q * T : (q + 1) * T])

    for h, tile in enumerate(tiles):
        cols = slice(h * T, (h + 1) * T)
        for dz, dy in sorted({offset_of(k)[:2] for k in ks}):
            some = [k for k in ks if offset_of(k)[:2] == (dz, dy)]
            start = origin + tile * T + ROW * dy + LAYER * dz
            window = xe[start : start + T, :].T
            if 13 in some:
                put(13, cols, window)
                some.remove(13)
            if len(some) > 1:
                pair = (some.pop(0), some.pop())
                right = [one_hot_columns(rel, k, first_tile + tile) for k in pair]
                put_dot(window, jnp.concatenate(right, axis=1), [(k, cols) for k in pair])
            for k in some:
                kept.append((k, cols, window, one_hot_columns(rel, k, first_tile + tile)))
            if len(kept) == 2:
                (k0, cols0, window0, hot0), (k1, cols1, window1, hot1) = kept
                right = jnp.concatenate(
                    [
                        jnp.concatenate([hot0, none], axis=1),
                        jnp.concatenate([none, hot1], axis=1),
                    ],
                    axis=0,
                )
                both = jnp.concatenate([window0, window1], axis=1)
                put_dot(both, right, [(k0, cols0), (k1, cols1)])
                kept = []
            yield
    for k, cols, window, hot in kept:
        put_dot(window, hot, [(k, cols)])


def weight_terms(chunks, ks_of, origin, f_ref, g_ref, xe, rel, buffers, acc):
    def product(chunk):
        here = slice(chunk * CHUNK_W, (chunk + 1) * CHUNK_W)
        picked_f, picked_g = buffers[chunk % 2]
        ks = ks_of(chunk)
        left_f, left_g = f_ref[here, :].T, g_ref[here, :].T
        if 13 in ks:
            picked_g[13 * T :, :] = left_g
        for left, picked, side, end in ((left_g, picked_f, 0, 13), (left_f, picked_g, 13, 14)):
            for group in (range(0, 4), range(4, 8), range(8, end)):
                group = [k for k in group if k in ks]
                if group:
                    span = slice(group[0] * T, (group[-1] + 1) * T)
                    to = slice((side + group[0]) * T, (side + group[-1] + 1) * T)
                    acc[:, to] += lax.dot_general(
                        left,
                        picked[span, :],
                        (((1,), (1,)), ((), ())),
                        preferred_element_type=jnp.float32,
                    )
                    yield

    pending = iter(())
    per = CHUNK_W // T
    for chunk in chunks:
        tiles = range(chunk * per, (chunk + 1) * per)
        ks = [k for k in ks_of(chunk) if k < 13]
        for _ in gather_columns(tiles, ks, xe, origin, rel, 0, *buffers[chunk % 2]):
            next(pending, None)
        for _ in pending:
            pass
        pending = product(chunk)
    for _ in pending:
        pass


def weight_inner_kernel(voxels, f_ref, g_ref, nb_ref, acc, xe, rel, gf, gg, gf2, gg2):
    channels = f_ref.shape[1]
    xe[ROW : ROW + voxels, 0:channels] = f_ref[...]
    xe[ROW : ROW + voxels, channels:] = g_ref[...]
    fill_edges(xe)
    for k in range(13):
        rel[k, :, :] = row_in_scene_window(nb_ref[k], ROW * offset_of(k)[1])
    acc[...] = jnp.zeros_like(acc)

    def ks_of(chunk):
        return range(9 if chunk < LAYER // CHUNK_W else 0, 14)

    chunks = range(voxels // CHUNK_W)
    weight_terms(chunks, ks_of, ROW, f_ref, g_ref, xe, rel, ((gf, gg), (gf2, gg2)), acc)


def weight_halo_kernel(scale, f_ref, g_ref, low_ref, nb_ref, in_ref, mine_ref, other_ref, xe, rel, gf, gg, gf2, gg2, acc, out_ref):
    channels = f_ref.shape[1]
    xe[ROW : ROW + LAYER, 0:channels] = low_ref[0]
    xe[ROW : ROW + LAYER, channels:] = low_ref[1]
    fill_edges(xe)
    for k in range(9):
        rel[k, :, :] = row_in_scene_window(nb_ref[k, 0 : LAYER // T, :], ROW * offset_of(k)[1])
    acc[...] = jnp.zeros_like(acc)
    chunks = range(LAYER // CHUNK_W)
    buffers = ((gf, gg), (gf2, gg2))
    weight_terms(chunks, lambda _: range(9), ROW + LAYER, f_ref, g_ref, xe, rel, buffers, acc)

    def total(block, touched):
        span = slice(block * T, (block + 1) * T)
        return (in_ref[:, span] + acc[:, span] if touched else in_ref[:, span]) * scale

    for k in range(13):
        out_ref[k * T : (k + 1) * T, :] = total(k, k < 9).T.astype(out_ref.dtype)
    for k in range(14):
        out_ref[(26 - k) * T : (27 - k) * T, :] = total(13 + k, k < 9).astype(out_ref.dtype)
    if out_ref.shape[0] > 27 * T:
        out_ref[27 * T :, :] = jnp.zeros((out_ref.shape[0] - 27 * T, out_ref.shape[1]), out_ref.dtype)
    half = out_ref.shape[0] // 2
    parity = own_side()
    mine_ref[...] = out_ref[pl.ds(pl.multiple_of(parity * half, 16), half), :]
    other_ref[...] = out_ref[pl.ds(pl.multiple_of((1 - parity) * half, 16), half), :]


def weight_scratch(rows, channels):
    return [
        pltpu.VMEM((rows + 2 * ROW, 2 * channels), jnp.bfloat16),
        pltpu.VMEM((13, rows // T, T), jnp.int32),
    ] + [
        pltpu.VMEM((13 * T, CHUNK_W), jnp.bfloat16),
        pltpu.VMEM((14 * T, CHUNK_W), jnp.bfloat16),
    ] * 2


def grad_w_inner(feats, grads, neigh):
    voxels, channels = feats.shape
    return pl.pallas_call(
        functools.partial(weight_inner_kernel, voxels),
        out_shape=jax.ShapeDtypeStruct((channels, 27 * T), jnp.float32),
        in_specs=[VMEM] * 3,
        out_specs=VMEM,
        scratch_shapes=weight_scratch(voxels, channels),
        compiler_params=pltpu.CompilerParams(vmem_limit_bytes=VMEM_LIMIT),
        cost_estimate=pl.CostEstimate(flops=8 * 10**9, bytes_accessed=4 * 10**6, transcendentals=0),
        name="weight_gradient_inner",
    )(feats, grads, neigh)


def grad_w_halo(feats, grads, low, neigh, partial, scale, rows):
    channels = feats.shape[1]
    out = jax.ShapeDtypeStruct((rows // 2, channels), jnp.bfloat16)
    return pl.pallas_call(
        functools.partial(weight_halo_kernel, scale),
        out_shape=(out, out),
        in_specs=[VMEM] * 5,
        out_specs=(VMEM, VMEM),
        scratch_shapes=weight_scratch(LAYER, channels)
        + [
            pltpu.VMEM((channels, 27 * T), jnp.float32),
            pltpu.VMEM((rows, channels), jnp.bfloat16),
        ],
        compiler_params=pltpu.CompilerParams(vmem_limit_bytes=VMEM_LIMIT),
        cost_estimate=pl.CostEstimate(flops=10**8, bytes_accessed=10**5, transcendentals=0),
        name="weight_gradient_halo",
    )(feats, grads, low, neigh, partial)


def stack_kernel(f_ref, g_ref, out_ref):
    out_ref[0] = f_ref[...]
    out_ref[1] = g_ref[...]


def stack_layer(feats, grads, layer, vmem, name):
    channels = feats.shape[1]
    block = pl.BlockSpec((LAYER, channels), lambda i: (layer, 0))
    return pl.pallas_call(
        stack_kernel,
        grid=(1,),
        out_shape=jax.ShapeDtypeStruct((2, LAYER, channels), jnp.bfloat16),
        in_specs=[block, block],
        out_specs=VMEM,
        compiler_params=pltpu.CompilerParams(vmem_limit_bytes=vmem),
        name=name,
    )(feats, grads)


def rows_needed(run):
    first, end = run
    return (
        first - LAYER - (ROW if first % LAYER else 0),
        end + LAYER + (ROW if end % LAYER else 0),
    )


def conv_kernel(voxels, run, halos, make_wt, f_ref, g_ref, nb_ref, w_hbm, *rest):
    halos = list(rest[:halos])
    if make_wt:
        conv_hbm, gin_hbm, wt_hbm, wt, w_ref, *scratch = rest[-15:]
    else:
        conv_hbm, gin_hbm, wt, *scratch = rest[-13:]
    conv_ref, gin_ref, xe, nb, rel, gf, gg, gf2, gg2, sems = scratch
    channels = f_ref.shape[1]
    size = run[1] - run[0]

    origin = run[0] - LAYER - ROW
    low, high = rows_needed(run)
    main = (max(low, 0), min(high, voxels))
    rows = pl.ds(main[0], main[1] - main[0])
    to = pl.ds(main[0] - origin, main[1] - main[0])
    copies = [
        (nb_ref, nb),
        (f_ref.at[rows, :], xe.at[to, pl.ds(0, channels)]),
        (g_ref.at[rows, :], xe.at[to, pl.ds(channels, channels)]),
    ]
    parts = []
    if low < 0:
        parts.append((pl.ds(LAYER + low, -low), pl.ds(low - origin, -low)))
    if high > voxels:
        parts.append((pl.ds(0, high - voxels), pl.ds(voxels - origin, high - voxels)))
    for halo, (rows, to) in zip(halos, parts):
        for side in range(2):
            lanes = pl.ds(side * channels, channels)
            copies.append((halo.at[side, rows, :], xe.at[to, lanes]))
    early = len(copies)
    copies.append((w_hbm, w_ref if make_wt else wt))
    copies = [
        pltpu.make_async_copy(source, target, sems.at[i])
        for i, (source, target) in enumerate(copies)
    ]
    for copy in copies:
        copy.start()
    edge = jnp.zeros((ROW, 2 * channels), jnp.bfloat16)
    if low - origin:
        xe[0:ROW, :] = edge
    if high - origin < xe.shape[0]:
        xe[xe.shape[0] - ROW :, :] = edge
    copies[0].wait()
    for k in range(27):
        rel[k, :, :] = row_in_scene_window(nb[k], ROW * offset_of(k)[1])
    for copy in copies[1:early]:
        copy.wait()

    buffers = ((gf, gg), (gf2, gg2))

    def product(chunk):
        rows = slice(chunk * CHUNK_C, (chunk + 1) * CHUNK_C)
        kernels = (slice(0, channels), slice(channels, 2 * channels))
        outs = ((conv_ref, conv_hbm), (gin_ref, gin_hbm))
        for (out, out_hbm), picked, side in zip(outs, buffers[chunk % 2], kernels):
            total = None
            for part in range(3):
                span = slice(part * 9 * T, (part + 1) * 9 * T)
                term = jnp.dot(wt[side, span], picked[span, :], preferred_element_type=jnp.float32)
                total = term if total is None else total + term
                if part == 2:
                    out[rows, :] = total.T.astype(jnp.bfloat16)
                    copy = pltpu.make_async_copy(
                        out.at[rows, :],
                        out_hbm.at[pl.ds(run[0] + chunk * CHUNK_C, CHUNK_C), :],
                        sems.at[len(copies) + len(written)],
                    )
                    copy.start()
                    written.append(copy)
                yield

    def turn_weights():
        copies[-1].wait()
        for k in range(27):
            span = slice(k * T, (k + 1) * T)
            wt[0:channels, span] = w_ref[span, :].T
            wt[channels:, span] = w_ref[(26 - k) * T : (27 - k) * T, :]
            if k % 2:
                yield
        copy = pltpu.make_async_copy(wt, wt_hbm, sems.at[len(copies)])
        copy.start()
        written.append(copy)

    written = []
    turning = turn_weights()
    pending = iter(())
    per = CHUNK_C // T
    for chunk in range(size // CHUNK_C):
        tiles = range(chunk * per, (chunk + 1) * per)
        center, first_tile = run[0] - origin, run[0] // T
        moves = gather_columns(
            tiles, range(27), xe, center, rel, first_tile, *buffers[chunk % 2]
        )
        for turn, _ in enumerate(moves):
            if turn % 3 == 2:
                next(pending, None)
            if chunk == 0 and make_wt and turn >= 4:
                next(turning, None)
        for _ in pending:
            pass
        if chunk == 0:
            if make_wt:
                for _ in turning:
                    pass
            else:
                copies[-1].wait()
        pending = product(chunk)
    for _ in pending:
        pass
    for copy in written:
        copy.wait()


def conv_run(feats, grads, low, high, neigh, weight, run, earlier, name):
    voxels, channels = feats.shape
    out = jax.ShapeDtypeStruct((voxels, channels), jnp.bfloat16)
    first, end = rows_needed(run)
    halos = ((low,) if first < 0 else ()) + ((high,) if end > voxels else ())
    turned = jax.ShapeDtypeStruct((2 * channels, 27 * channels), jnp.bfloat16)
    make_wt = not earlier
    operands = (feats, grads, neigh, weight if make_wt else earlier[2]) + halos + earlier[:2]
    size = run[1] - run[0]
    results = pl.pallas_call(
        functools.partial(conv_kernel, voxels, run, len(halos), make_wt),
        out_shape=(out, out) + ((turned,) if make_wt else ()),
        in_specs=[HBM] * len(operands),
        out_specs=(HBM, HBM) + ((HBM,) if make_wt else ()),
        input_output_aliases={4 + len(halos) + i: i for i in range(len(earlier[:2]))},
        scratch_shapes=[
            pltpu.VMEM(turned.shape, jnp.bfloat16),
        ]
        + ([pltpu.VMEM(weight.shape, jnp.bfloat16)] if make_wt else [])
        + [
            pltpu.VMEM((size, channels), jnp.bfloat16),
            pltpu.VMEM((size, channels), jnp.bfloat16),
            pltpu.VMEM((size + 2 * (LAYER + ROW), 2 * channels), jnp.bfloat16),
            pltpu.VMEM(neigh.shape, jnp.int32),
            pltpu.VMEM(neigh.shape, jnp.int32),
        ]
        + [pltpu.VMEM((27 * T, CHUNK_C), jnp.bfloat16)] * 4
        + [pltpu.SemaphoreType.DMA((8 + 2 * size // CHUNK_C,))],
        compiler_params=pltpu.CompilerParams(vmem_limit_bytes=FULL_VMEM_LIMIT),
        cost_estimate=pl.CostEstimate(
            flops=10**8 if make_wt else 10**10, bytes_accessed=10**5, transcendentals=0
        ),
        name=name,
    )(*operands)
    return tuple(results) + earlier[2:]


def sum_kernel(*refs):
    *parts, out_ref = refs
    terms = [ref[i] for ref in parts for i in range(ref.shape[0])]
    total = terms[0].astype(jnp.float32)
    for term in terms[1:]:
        total += term.astype(jnp.float32)
    total = total.astype(out_ref.dtype)
    for i in range(out_ref.shape[0]):
        out_ref[i] = total


def sum_parts(parts, copies, name):
    shape = parts[0].shape[1:]
    return pl.pallas_call(
        sum_kernel,
        out_shape=jax.ShapeDtypeStruct((copies,) + shape, parts[0].dtype),
        in_specs=[VMEM] * len(parts),
        out_specs=VMEM,
        compiler_params=pltpu.CompilerParams(vmem_limit_bytes=VMEM_LIMIT),
        name=name,
    )(*parts)


def widen_kernel(in_ref, *rest):
    out_ref = rest[-1]
    out_ref[...] = in_ref[...].astype(out_ref.dtype)


def widen(rows, own, count, earlier, name):
    half, channels = rows.shape
    block = (half // 2, channels)

    def place(i):
        side = own_side() if own else 1 - own_side()
        return side * 2 + i, 0

    return pl.pallas_call(
        widen_kernel,
        grid=(2,),
        in_specs=[pl.BlockSpec(block, lambda i: (i, 0))]
        + [pl.BlockSpec(memory_space=pl.ANY)] * len(earlier),
        out_specs=pl.BlockSpec(block, place),
        out_shape=jax.ShapeDtypeStruct((count, channels), jnp.float32),
        input_output_aliases={1 + i: i for i in range(len(earlier))},
        compiler_params=pltpu.CompilerParams(vmem_limit_bytes=VMEM_LIMIT),
        name=name,
    )(rows, *earlier)


def local(features, neighbours, weight, grad_out):
    feats, grads = features[0], grad_out[0]
    voxels, channels = feats.shape
    neigh = neighbours.reshape(27, voxels // T, T)
    space, dp = lax.axis_size("space"), lax.axis_size("dp")
    up = [(i, i + 1) for i in range(space - 1)]
    down = [(i + 1, i) for i in range(space - 1)]
    low = lax.ppermute(
        stack_layer(feats, grads, voxels // LAYER - 1, FULL_VMEM_LIMIT, "stack_last_layer"), "space", up
    )

    scale = 1.0 / math.sqrt(dp * space * voxels)
    share = -(-27 * channels // (16 * dp)) * 16
    inner = grad_w_inner(feats, grads, neigh)
    inner, later_feats, later_grads = lax.optimization_barrier((inner, feats, grads))
    first = stack_layer(later_feats, later_grads, 0, VMEM_LIMIT, "stack_first_layer")
    high = lax.ppermute(first, "space", down)
    inner, first = lax.optimization_barrier((inner, first))
    mine, other = grad_w_halo(feats, grads, low, neigh, inner, scale, share * dp)
    swap = [(i, i ^ 1) for i in range(dp)]
    alike = [list(range(0, dp, 2)), list(range(1, dp, 2))]
    other = lax.ppermute(other, "dp", swap)
    mine = sum_parts((mine[None], other[None]), 1, "sum_of_pair")
    mine, flat_weight = lax.optimization_barrier(
        (mine, weight.reshape(27 * channels, channels))
    )
    chunks = voxels // CHUNK_C
    ends = [0, chunks // 4 * CHUNK_C, chunks * 3 // 4 * CHUNK_C, voxels]

    def conv(done, part):
        run = (ends[part], ends[part + 1])
        name = "conv_run_%d" % part
        return conv_run(feats, grads, low, high, neigh, flat_weight, run, done, name)

    def exchange(pieces):
        return lax.all_to_all(pieces, "dp", 0, 0, axis_index_groups=alike, tiled=True)

    pieces = exchange(mine.reshape(dp // 2, share, channels))
    done = conv((), 0)
    pieces, done = lax.optimization_barrier((pieces, done))
    pieces = lax.all_to_all(sum_parts((pieces,), space, "sum_for_space"), "space", 0, 0, tiled=True)
    done = conv(done, 1)
    pieces, done = lax.optimization_barrier((pieces, done))
    pieces = exchange(sum_parts((pieces,), dp // 2, "sum_for_dp"))
    done = conv(done, 2)
    pieces, done = lax.optimization_barrier((pieces, done))
    mine = pieces.reshape(dp // 2 * share, channels)
    other = lax.ppermute(mine, "dp", swap)
    grad_w = widen(mine, True, 27 * channels, (), "widen_own_half")
    grad_w = widen(other, False, 27 * channels, (grad_w,), "widen_other_half")
    conv_out, grad_in, _ = done
    return conv_out[None], grad_in[None], grad_w.reshape(27, channels, channels)


def solution(mesh):
    in_specs = (P("dp", "space", None), P("dp", None, "space"), P(), P("dp", "space", None))
    out_specs = (P("dp", "space", None), P("dp", "space", None), P())
    return jax.shard_map(local, mesh=mesh, in_specs=in_specs, out_specs=out_specs, check_vma=False)
```

profile of v0, /device:TPU:0, one launch (start us, length us, event | category | flops | bytes accessed | tf_op | source)
XLA Modules:
  0.0 69.7 jit_solution(5354001575870516733)
XLA Ops:
  0.6 0.0 copy-start.1
  0.6 0.0 copy-start
  0.7 0.0 copy-start.3
  0.7 2.0 %stack_last_layer.1 = bf16[2,1024,128]{2,1,0:T(8,128)(2,1)} custom-call(bf16[3072,128]{1,0:T(8,128)(2,1)} %bitcast.11, bf16[3072,128]{1,0:T(8,128)(2,1)} %bitcast.18), custom_call_target="tpu_custom_call" | custom-call | tf_op jit(solution)/shard_map/stack_last_layer/pallas_call | solution.py:228
  2.7 4.9 %collective-permute-start = (bf16[2,1024,128]{2,1,0:T(8,128)(2,1)}, bf16[2,1024,128]{2,1,0:T(8,128)(2,1)S(1)}, u32[]{:S(2)}, u32[]{:S(2)}) collective-permute-start(bf16[2,1024,128]{2,1,0:T(8,128)(2,1)} %stack_last_layer.1), channel_id=1, source_target_pairs={{0,1},{1,2},{2,3},{4,5},{5,6},{6,7},{8,9},{9,10},{10,11},{12,13},{... | collective-permute-start | bytes 1572872 | tf_op jit(solution)/shard_map/ppermute | solution.py:453
  7.6 0.0 copy-done.1
  7.6 0.0 copy-done
  7.6 0.0 copy-done.3
  7.6 8.0 %weight_gradient_inner.1.in_ref = f32[128,3456]{1,0:T(8,128)S(1)} custom-call(bf16[3072,128]{1,0:T(8,128)(2,1)S(1)} %bitcast.15, bf16[3072,128]{1,0:T(8,128)(2,1)S(1)} %bitcast.22, s32[27,24,128]{2,1,0:T(8,128)S(1)} %bitcast.30), custom_call_target="tpu_custom_call" | custom-call | flops 8000000000 | bytes 4000000 | tf_op jit(solution)/shard_map/weight_gradient_inner/pallas_call | solution.py:189
  15.7 3.3 %collective-permute-done.low_ref.rest_0_ = bf16[2,1024,128]{2,1,0:T(8,128)(2,1)S(1)} collective-permute-done((bf16[2,1024,128]{2,1,0:T(8,128)(2,1)}, bf16[2,1024,128]{2,1,0:T(8,128)(2,1)S(1)}, u32[]{:S(2)}, u32[]{:S(2)}) %collective-permute-start) | collective-permute-done | bytes 524320 | tf_op jit(solution)/shard_map/ppermute | solution.py:453
  19.1 0.0 copy-start.2
  19.1 2.7 %weight_gradient_halo.1 = (bf16[1728,128]{1,0:T(8,128)(2,1)S(1)}, bf16[1728,128]{1,0:T(8,128)(2,1)S(1)}) custom-call(bf16[3072,128]{1,0:T(8,128)(2,1)S(1)} %bitcast.17, bf16[3072,128]{1,0:T(8,128)(2,1)S(1)} %bitcast.24, bf16[2,1024,128]{2,1,0:T(8,128)(2,1)S(1)} %collective-permute-done.low_ref.rest_0_, s32[27,24,128]{2,1,0:T(8,128)S(1)} %bitcast.31, ...), custom_call_target="tpu_custom_call" | custom-call | flops 100000000 | bytes 100000 | tf_op jit(solution)/shard_map/weight_gradient_halo/pallas_call | solution.py:204
  21.7 0.0 copy-done.2
  21.7 0.1 collective-permute-start.1
  21.8 1.3 %collective-permute-start.2 = (bf16[2,1024,128]{2,1,0:T(8,128)(2,1)S(1)}, bf16[2,1024,128]{2,1,0:T(8,128)(2,1)S(1)}, u32[]{:S(2)}, u32[]{:S(2)}) collective-permute-start(bf16[2,1024,128]{2,1,0:T(8,128)(2,1)S(1)} %stack_first_layer.1), channel_id=1, source_target_pairs={{1,0},{2,1},{3,2},{5,4},{6,5},{7,6},{9,8},{10,9},{11,10},{13,12},{... | collective-permute-start | bytes 1572872 | tf_op jit(solution)/shard_map/ppermute | solution.py:462
  23.1 0.5 collective-permute-done.1
  23.6 0.9 %sum_of_pair.1 = bf16[1,1728,128]{2,1,0:T(8,128)(2,1)} custom-call(bf16[1,1728,128]{2,1,0:T(8,128)(2,1)S(1)} %bitcast.32, bf16[1,1728,128]{2,1,0:T(8,128)(2,1)S(1)} %bitcast.33), custom_call_target="tpu_custom_call" | custom-call | tf_op jit(solution)/shard_map/sum_of_pair/pallas_call | solution.py:410
  24.4 3.7 %all-to-all-start = ((bf16[4,432,128]{2,1,0:T(8,128)(2,1)}), bf16[4,432,128]{2,1,0:T(8,128)(2,1)S(1)}, u32[]{:S(2)}, u32[]{:S(2)}) async-start(bf16[4,432,128]{2,1,0:T(8,128)(2,1)} %bitcast.6), calls=%async_computation | async-start | bytes 884736 | tf_op jit(solution)/shard_map/all_to_all | solution.py:481
  28.2 7.0 %conv_run_0.1 = (bf16[3072,128]{1,0:T(8,128)(2,1)}, bf16[3072,128]{1,0:T(8,128)(2,1)}, bf16[256,3456]{1,0:T(8,128)(2,1)}) custom-call(bf16[3072,128]{1,0:T(8,128)(2,1)} %bitcast.12, bf16[3072,128]{1,0:T(8,128)(2,1)} %bitcast.19, s32[27,24,128]{2,1,0:T(8,128)} %bitcast.27, bf16[3456,128]{1,0:T(8,128)(2,1)} %bitcast.35, bf16[2,1024,128]{2,1,0:T(8,128)(2,1)} %copy-done.2), custom_call_target="tpu_custom_call" | custom-call | flops 100000000 | bytes 100000 | tf_op jit(solution)/shard_map/conv_run_0/pallas_call | solution.py:369
  35.2 0.4 all-to-all-done.refs_0_
  35.6 0.9 %sum_for_space.1 = bf16[4,432,128]{2,1,0:T(8,128)(2,1)} custom-call(bf16[4,432,128]{2,1,0:T(8,128)(2,1)S(1)} %all-to-all-done.refs_0_), custom_call_target="tpu_custom_call" | custom-call | tf_op jit(solution)/shard_map/sum_for_space/pallas_call | solution.py:410
  36.5 6.4 %all-to-all-start.1 = ((bf16[4,432,128]{2,1,0:T(8,128)(2,1)}), bf16[4,432,128]{2,1,0:T(8,128)(2,1)S(1)}, u32[]{:S(2)}, u32[]{:S(2)}) async-start(bf16[4,432,128]{2,1,0:T(8,128)(2,1)} %sum_for_space.1), calls=%async_computation.1 | async-start | bytes 884736 | tf_op jit(solution)/shard_map/all_to_all | solution.py:486
  42.8 0.0 collective-permute-done.2.rest_1_.rest_0_
  42.8 0.0 copy-start.4
  42.8 0.8 %copy-done.4 = bf16[2,1024,128]{2,1,0:T(8,128)(2,1)} copy-done((bf16[2,1024,128]{2,1,0:T(8,128)(2,1)}, bf16[2,1024,128]{2,1,0:T(8,128)(2,1)S(1)}, u32[]{:S(2)}) %copy-start.4) | copy-done | bytes 524312
  43.6 11.3 %conv_run_1.1 = (bf16[3072,128]{1,0:T(8,128)(2,1)}, bf16[3072,128]{1,0:T(8,128)(2,1)}) custom-call(bf16[3072,128]{1,0:T(8,128)(2,1)} %bitcast.13, bf16[3072,128]{1,0:T(8,128)(2,1)} %bitcast.20, s32[27,24,128]{2,1,0:T(8,128)} %bitcast.28, bf16[256,3456]{1,0:T(8,128)(2,1)} %get-tuple-element.47.w_hbm, ...), custom_call_target="tpu_custom_call", output_to_operand_aliasing={{0}: (6, {}), {1}: (7, {})} | custom-call | flops 10000000000 | bytes 100000 | tf_op jit(solution)/shard_map/conv_run_1/pallas_call | solution.py:369
  55.0 0.4 all-to-all-done.1.refs_0_
  55.4 0.8 %sum_for_dp.1 = bf16[4,432,128]{2,1,0:T(8,128)(2,1)} custom-call(bf16[4,432,128]{2,1,0:T(8,128)(2,1)S(1)} %all-to-all-done.1.refs_0_), custom_call_target="tpu_custom_call" | custom-call | tf_op jit(solution)/shard_map/sum_for_dp/pallas_call | solution.py:410
  56.2 3.7 %all-to-all-start.2 = ((bf16[4,432,128]{2,1,0:T(8,128)(2,1)}), bf16[4,432,128]{2,1,0:T(8,128)(2,1)S(1)}, u32[]{:S(2)}, u32[]{:S(2)}) async-start(bf16[4,432,128]{2,1,0:T(8,128)(2,1)} %sum_for_dp.1), calls=%async_computation.2 | async-start | bytes 884736 | tf_op jit(solution)/shard_map/all_to_all | solution.py:481
  59.9 6.9 %conv_run_2.1 = (bf16[3072,128]{1,0:T(8,128)(2,1)}, bf16[3072,128]{1,0:T(8,128)(2,1)}) custom-call(bf16[3072,128]{1,0:T(8,128)(2,1)} %bitcast.14, bf16[3072,128]{1,0:T(8,128)(2,1)} %bitcast.21, s32[27,24,128]{2,1,0:T(8,128)} %bitcast.29, bf16[256,3456]{1,0:T(8,128)(2,1)} %get-tuple-element.47.w_hbm, ...), custom_call_target="tpu_custom_call", output_to_operand_aliasing={{0}: (5, {}), {1}: (6, {})} | custom-call | flops 10000000000 | bytes 100000 | tf_op jit(solution)/shard_map/conv_run_2/pallas_call | solution.py:369
  66.9 0.0 all-to-all-done.2
  66.9 0.1 collective-permute-start.3
  67.0 1.0 %widen_own_half.1.rest_0_ = f32[3456,128]{1,0:T(8,128)} custom-call(bf16[1728,128]{1,0:T(8,128)(2,1)S(1)} %bitcast.26), custom_call_target="tpu_custom_call" | custom-call | tf_op jit(solution)/shard_map/widen_own_half/pallas_call | solution.py:433
  67.9 0.8 %collective-permute-done.3.in_ref = bf16[1728,128]{1,0:T(8,128)(2,1)S(1)} collective-permute-done((bf16[1728,128]{1,0:T(8,128)(2,1)S(1)}, bf16[1728,128]{1,0:T(8,128)(2,1)S(1)}, u32[]{:S(2)}, u32[]{:S(2)}) %collective-permute-start.3) | collective-permute-done | bytes 442400 | tf_op jit(solution)/shard_map/ppermute | solution.py:493
  68.7 0.9 %widen_other_half.1 = f32[3456,128]{1,0:T(8,128)} custom-call(bf16[1728,128]{1,0:T(8,128)(2,1)S(1)} %collective-permute-done.3.in_ref, f32[3456,128]{1,0:T(8,128)} %widen_own_half.1.rest_0_), custom_call_target="tpu_custom_call", output_to_operand_aliasing={{}: (1, {})} | custom-call | tf_op jit(solution)/shard_map/widen_other_half/pallas_call | solution.py:433
  (1 shorter events, 0.0 us)
Async XLA Ops:
  0.6 7.0 %copy-start.1 = (bf16[1,3072,128]{2,1,0:T(8,128)(2,1)S(1)}, bf16[1,3072,128]{2,1,0:T(8,128)(2,1)}, u32[]{:S(2)}) copy-start(bf16[1,3072,128]{2,1,0:T(8,128)(2,1)} %param.7) | copy-start | bytes 2359300
  0.6 7.0 %copy-start = (bf16[1,3072,128]{2,1,0:T(8,128)(2,1)S(1)}, bf16[1,3072,128]{2,1,0:T(8,128)(2,1)}, u32[]{:S(2)}) copy-start(bf16[1,3072,128]{2,1,0:T(8,128)(2,1)} %param.4) | copy-start | bytes 2359300
  0.7 7.0 %copy-start.3 = (s32[1,27,3072]{2,0,1:T(1,128)S(1)}, s32[1,27,3072]{2,0,1:T(1,128)}, u32[]{:S(2)}) copy-start(s32[1,27,3072]{2,0,1:T(1,128)} %param.5) | copy-start | bytes 995332
  2.7 16.4 %collective-permute-start = (bf16[2,1024,128]{2,1,0:T(8,128)(2,1)}, bf16[2,1024,128]{2,1,0:T(8,128)(2,1)S(1)}, u32[]{:S(2)}, u32[]{:S(2)}) collective-permute-start(bf16[2,1024,128]{2,1,0:T(8,128)(2,1)} %stack_last_layer.1), channel_id=1, source_target_pairs={{0,1},{1,2},{2,3},{4,5},{5,6},{6,7},{8,9},{9,10},{10,11},{12,13},{... | collective-permute-start | bytes 1572872 | tf_op jit(solution)/shard_map/ppermute | solution.py:453
  19.1 2.7 %copy-start.2 = (bf16[2,1024,128]{2,1,0:T(8,128)(2,1)}, bf16[2,1024,128]{2,1,0:T(8,128)(2,1)S(1)}, u32[]{:S(2)}) copy-start(bf16[2,1024,128]{2,1,0:T(8,128)(2,1)S(1)} %collective-permute-done.low_ref.rest_0_) | copy-start | bytes 1572868
  21.7 1.9 %collective-permute-start.1 = (bf16[1728,128]{1,0:T(8,128)(2,1)S(1)}, bf16[1728,128]{1,0:T(8,128)(2,1)S(1)}, u32[]{:S(2)}, u32[]{:S(2)}) collective-permute-start(bf16[1728,128]{1,0:T(8,128)(2,1)S(1)} %get-tuple-element.34), channel_id=1, source_target_pairs={{0,4},{4,0},{8,12},{12,8},{16,20},{20,16},{24,28},{28,24},{1,5},{5... | collective-permute-start | bytes 1327112 | tf_op jit(solution)/shard_map/ppermute | solution.py:467
  21.8 21.0 %collective-permute-start.2 = (bf16[2,1024,128]{2,1,0:T(8,128)(2,1)S(1)}, bf16[2,1024,128]{2,1,0:T(8,128)(2,1)S(1)}, u32[]{:S(2)}, u32[]{:S(2)}) collective-permute-start(bf16[2,1024,128]{2,1,0:T(8,128)(2,1)S(1)} %stack_first_layer.1), channel_id=1, source_target_pairs={{1,0},{2,1},{3,2},{5,4},{6,5},{7,6},{9,8},{10,9},{11,10},{13,12},{... | collective-permute-start | bytes 1572872 | tf_op jit(solution)/shard_map/ppermute | solution.py:462
  24.4 11.2 %all-to-all-start = ((bf16[4,432,128]{2,1,0:T(8,128)(2,1)}), bf16[4,432,128]{2,1,0:T(8,128)(2,1)S(1)}, u32[]{:S(2)}, u32[]{:S(2)}) async-start(bf16[4,432,128]{2,1,0:T(8,128)(2,1)} %bitcast.6), calls=%async_computation | async-start | bytes 884736 | tf_op jit(solution)/shard_map/all_to_all | solution.py:481
  36.5 18.9 %all-to-all-start.1 = ((bf16[4,432,128]{2,1,0:T(8,128)(2,1)}), bf16[4,432,128]{2,1,0:T(8,128)(2,1)S(1)}, u32[]{:S(2)}, u32[]{:S(2)}) async-start(bf16[4,432,128]{2,1,0:T(8,128)(2,1)} %sum_for_space.1), calls=%async_computation.1 | async-start | bytes 884736 | tf_op jit(solution)/shard_map/all_to_all | solution.py:486
  42.8 0.8 %copy-start.4 = (bf16[2,1024,128]{2,1,0:T(8,128)(2,1)}, bf16[2,1024,128]{2,1,0:T(8,128)(2,1)S(1)}, u32[]{:S(2)}) copy-start(bf16[2,1024,128]{2,1,0:T(8,128)(2,1)S(1)} %collective-permute-done.2.rest_1_.rest_0_) | copy-start | bytes 1572868
  56.2 10.6 %all-to-all-start.2 = ((bf16[4,432,128]{2,1,0:T(8,128)(2,1)}), bf16[4,432,128]{2,1,0:T(8,128)(2,1)S(1)}, u32[]{:S(2)}, u32[]{:S(2)}) async-start(bf16[4,432,128]{2,1,0:T(8,128)(2,1)} %sum_for_dp.1), calls=%async_computation.2 | async-start | bytes 884736 | tf_op jit(solution)/shard_map/all_to_all | solution.py:481
  66.9 1.9 %collective-permute-start.3 = (bf16[1728,128]{1,0:T(8,128)(2,1)S(1)}, bf16[1728,128]{1,0:T(8,128)(2,1)S(1)}, u32[]{:S(2)}, u32[]{:S(2)}) collective-permute-start(bf16[1728,128]{1,0:T(8,128)(2,1)S(1)} %bitcast.25), channel_id=1, source_target_pairs={{0,4},{4,0},{8,12},{12,8},{16,20},{20,16},{24,28},{28,24},{1,5},{5... | collective-permute-start | bytes 1327112 | tf_op jit(solution)/shard_map/ppermute | solution.py:493
where the time goes:
time: 70.1 us; the launch traced here: 69.7 us
  Pallas kernels  42.4 us (60%)
  starting transfers between devices  20.2 us (29%)
  waiting for transfers between devices  5.48 us (8%)
  local copies, waits for them, and re-layouts  0.82 us (1%)
  between operations  0.77 us (1%)
    pallas_call x3, Pallas kernels, conv_run(): pl.pallas_call(functools.partial(conv_kernel, voxels, run, len(halos), ma...  25.2 us
    pallas_call x1, Pallas kernels, grad_w_inner(): pl.pallas_call(functools.partial(weight_inner_kernel, voxels), out_shape=...  8.04 us
    all_to_all x2, starting transfers between devices, exchange(): lax.all_to_all(pieces, 'dp', 0, 0, axis_index_groups=alike, tiled=True)  7.43 us
    all_to_all x1, starting transfers between devices, local(): lax.all_to_all(sum_parts((pieces,), space, 'sum_for_space'), 'space', 0,...  6.37 us
    ppermute x1, starting transfers between devices, local(): lax.ppermute(stack_layer(feats, grads, voxels // LAYER - 1, FULL_VMEM_LIM...  4.95 us
    ppermute x1, waiting for transfers between devices, local(): lax.ppermute(stack_layer(feats, grads, voxels // LAYER - 1, FULL_VMEM_LIM...  3.33 us
    pallas_call x1, Pallas kernels, grad_w_halo(): pl.pallas_call(functools.partial(weight_halo_kernel, scale), out_shape=(o...  2.66 us
    pallas_call x3, Pallas kernels, sum_parts(): pl.pallas_call(sum_kernel, out_shape=jax.ShapeDtypeStruct((copies,) + sha...  2.55 us
  transfers between devices with their start and end apart: 7, of which 5 were waited for; matrix products, arithmetic and copies ran while one was open for 0% of the time, Pallas kernels for 52%

commit v1 on v0

--- a/solution.py
+++ b/solution.py
@@ -212,7 +212,7 @@
             pltpu.VMEM((rows, channels), jnp.bfloat16),
         ],
         compiler_params=pltpu.CompilerParams(vmem_limit_bytes=VMEM_LIMIT),
-        cost_estimate=pl.CostEstimate(flops=10**8, bytes_accessed=10**5, transcendentals=0),
+        cost_estimate=pl.CostEstimate(flops=10**6, bytes_accessed=10**4, transcendentals=0),
         name="weight_gradient_halo",
     )(feats, grads, low, neigh, partial)
 
@@ -387,7 +387,7 @@
         + [pltpu.SemaphoreType.DMA((8 + 2 * size // CHUNK_C,))],
         compiler_params=pltpu.CompilerParams(vmem_limit_bytes=FULL_VMEM_LIMIT),
         cost_estimate=pl.CostEstimate(
-            flops=10**8 if make_wt else 10**10, bytes_accessed=10**5, transcendentals=0
+            flops=10**6 if make_wt else 10**10, bytes_accessed=10**4, transcendentals=0
         ),
         name=name,
     )(*operands)
@@ -413,6 +413,7 @@
         in_specs=[VMEM] * len(parts),
         out_specs=VMEM,
         compiler_params=pltpu.CompilerParams(vmem_limit_bytes=VMEM_LIMIT),
+        cost_estimate=pl.CostEstimate(flops=10**6, bytes_accessed=10**4, transcendentals=0),
         name=name,
     )(*parts)
 
@@ -481,6 +482,7 @@
         return lax.all_to_all(pieces, "dp", 0, 0, axis_index_groups=alike, tiled=True)
 
     pieces = exchange(mine.reshape(dp // 2, share, channels))
+    flat_weight, high = lax.optimization_barrier((flat_weight, high))
     done = conv((), 0)
     pieces, done = lax.optimization_barrier((pieces, done))
     pieces = lax.all_to_all(sum_parts((pieces,), space, "sum_for_space"), "space", 0, 0, tiled=True)

time: 70.1 us -> 78 us (1.11)
  waiting for transfers between devices: 5.48 us -> 16.4 us
  starting transfers between devices: 20.2 us -> 17.8 us
  local copies, waits for them, and re-layouts: 0.82 us -> 0.03 us
    ppermute x1, waiting for transfers between devices: 0.01 us -> 10.4 us  [local(): high = lax.ppermute(first, 'space', down)]
    all_to_all x1, starting transfers between devices: 6.37 us -> 4.02 us  [local(): lax.all_to_all(sum_parts((pieces,), space, 'sum_for_space'), 'space', 0,...]
    all_to_all x1, waiting for transfers between devices: 0.43 us -> 1.29 us  [local(): lax.all_to_all(sum_parts((pieces,), space, 'sum_for_space'), 'space', 0,...]
    unnamed x10, local copies, waits for them, and re-layouts: 0.82 us -> 0.03 us
  transfers between devices with their start and end apart: 7 -> 7, of which waited for: 5 -> 5; matrix products, arithmetic and copies ran while one was open for 0% -> 0% of each run, Pallas kernels for 52% -> 46%
where the time goes in v1:
time: 78 us; the launch traced here: 77.6 us
  Pallas kernels  42.6 us (55%)
  starting transfers between devices  17.8 us (23%)
  waiting for transfers between devices  16.4 us (21%)
    pallas_call x3, Pallas kernels, conv_run(): pl.pallas_call(functools.partial(conv_kernel, voxels, run, len(halos), ma...  25.4 us
    ppermute x1, waiting for transfers between devices, local(): high = lax.ppermute(first, 'space', down)  10.4 us
    pallas_call x1, Pallas kernels, grad_w_inner(): pl.pallas_call(functools.partial(weight_inner_kernel, voxels), out_shape=...  8.04 us
    all_to_all x2, starting transfers between devices, exchange(): lax.all_to_all(pieces, 'dp', 0, 0, axis_index_groups=alike, tiled=True)  7.44 us
    ppermute x1, starting transfers between devices, local(): lax.ppermute(stack_layer(feats, grads, voxels // LAYER - 1, FULL_VMEM_LIM...  4.95 us
    all_to_all x1, starting transfers between devices, local(): lax.all_to_all(sum_parts((pieces,), space, 'sum_for_space'), 'space', 0,...  4.02 us
    ppermute x1, waiting for transfers between devices, local(): lax.ppermute(stack_layer(feats, grads, voxels // LAYER - 1, FULL_VMEM_LIM...  3.33 us
    pallas_call x1, Pallas kernels, grad_w_halo(): pl.pallas_call(functools.partial(weight_halo_kernel, scale), out_shape=(o...  2.66 us
  transfers between devices with their start and end apart: 7, of which 5 were waited for; matrix products, arithmetic and copies ran while one was open for 0% of the time, Pallas kernels for 46%

profile of v1, /device:TPU:0, one launch (start us, length us, event | category | flops | bytes accessed | tf_op | source)
XLA Modules:
  0.0 77.6 jit_solution(14680509248833798774)
XLA Ops:
  0.6 0.0 copy-start.1
  0.6 0.0 copy-start
  0.7 0.0 copy-start.3
  0.7 2.0 %stack_last_layer.1 = bf16[2,1024,128]{2,1,0:T(8,128)(2,1)} custom-call(bf16[3072,128]{1,0:T(8,128)(2,1)} %bitcast.11, bf16[3072,128]{1,0:T(8,128)(2,1)} %bitcast.18), custom_call_target="tpu_custom_call" | custom-call | tf_op jit(solution)/shard_map/stack_last_layer/pallas_call | solution.py:228
  2.7 4.9 %collective-permute-start = (bf16[2,1024,128]{2,1,0:T(8,128)(2,1)}, bf16[2,1024,128]{2,1,0:T(8,128)(2,1)S(1)}, u32[]{:S(2)}, u32[]{:S(2)}) collective-permute-start(bf16[2,1024,128]{2,1,0:T(8,128)(2,1)} %stack_last_layer.1), channel_id=1, source_target_pairs={{0,1},{1,2},{2,3},{4,5},{5,6},{6,7},{8,9},{9,10},{10,11},{12,13},{... | collective-permute-start | bytes 1572872 | tf_op jit(solution)/shard_map/ppermute | solution.py:454
  7.6 0.0 copy-done.1
  7.6 0.0 copy-done
  7.6 0.0 copy-done.3
  7.6 8.0 %weight_gradient_inner.1.in_ref = f32[128,3456]{1,0:T(8,128)S(1)} custom-call(bf16[3072,128]{1,0:T(8,128)(2,1)S(1)} %bitcast.15, bf16[3072,128]{1,0:T(8,128)(2,1)S(1)} %bitcast.22, s32[27,24,128]{2,1,0:T(8,128)S(1)} %bitcast.30), custom_call_target="tpu_custom_call" | custom-call | flops 8000000000 | bytes 4000000 | tf_op jit(solution)/shard_map/weight_gradient_inner/pallas_call | solution.py:189
  15.7 3.3 %collective-permute-done.low_ref.rest_0_ = bf16[2,1024,128]{2,1,0:T(8,128)(2,1)S(1)} collective-permute-done((bf16[2,1024,128]{2,1,0:T(8,128)(2,1)}, bf16[2,1024,128]{2,1,0:T(8,128)(2,1)S(1)}, u32[]{:S(2)}, u32[]{:S(2)}) %collective-permute-start) | collective-permute-done | bytes 524320 | tf_op jit(solution)/shard_map/ppermute | solution.py:454
  19.1 0.0 copy-start.2
  19.1 2.7 %weight_gradient_halo.1 = (bf16[1728,128]{1,0:T(8,128)(2,1)S(1)}, bf16[1728,128]{1,0:T(8,128)(2,1)S(1)}) custom-call(bf16[3072,128]{1,0:T(8,128)(2,1)S(1)} %bitcast.17, bf16[3072,128]{1,0:T(8,128)(2,1)S(1)} %bitcast.24, bf16[2,1024,128]{2,1,0:T(8,128)(2,1)S(1)} %collective-permute-done.low_ref.rest_0_, s32[27,24,128]{2,1,0:T(8,128)S(1)} %bitcast.31, ...), custom_call_target="tpu_custom_call" | custom-call | flops 1000000 | bytes 10000 | tf_op jit(solution)/shard_map/weight_gradient_halo/pallas_call | solution.py:204
  21.7 0.0 copy-done.2
  21.7 0.1 collective-permute-start.1
  21.8 1.3 %collective-permute-start.2 = (bf16[2,1024,128]{2,1,0:T(8,128)(2,1)S(1)}, bf16[2,1024,128]{2,1,0:T(8,128)(2,1)S(1)}, u32[]{:S(2)}, u32[]{:S(2)}) collective-permute-start(bf16[2,1024,128]{2,1,0:T(8,128)(2,1)S(1)} %stack_first_layer.1), channel_id=1, source_target_pairs={{1,0},{2,1},{3,2},{5,4},{6,5},{7,6},{9,8},{10,9},{11,10},{13,12},{... | collective-permute-start | bytes 1572872 | tf_op jit(solution)/shard_map/ppermute | solution.py:463
  23.1 0.5 collective-permute-done.1
  23.6 0.9 %sum_of_pair.1 = bf16[1,1728,128]{2,1,0:T(8,128)(2,1)} custom-call(bf16[1,1728,128]{2,1,0:T(8,128)(2,1)S(1)} %bitcast.32, bf16[1,1728,128]{2,1,0:T(8,128)(2,1)S(1)} %bitcast.33), custom_call_target="tpu_custom_call" | custom-call | flops 1000000 | bytes 10000 | tf_op jit(solution)/shard_map/sum_of_pair/pallas_call | solution.py:410
  24.5 3.7 %all-to-all-start = ((bf16[4,432,128]{2,1,0:T(8,128)(2,1)}), bf16[4,432,128]{2,1,0:T(8,128)(2,1)S(1)}, u32[]{:S(2)}, u32[]{:S(2)}) async-start(bf16[4,432,128]{2,1,0:T(8,128)(2,1)} %bitcast.6), calls=%async_computation | async-start | bytes 884736 | tf_op jit(solution)/shard_map/all_to_all | solution.py:482
  28.2 10.4 %collective-permute-done.2.rest_1_.rest_0_ = bf16[2,1024,128]{2,1,0:T(8,128)(2,1)S(1)} collective-permute-done((bf16[2,1024,128]{2,1,0:T(8,128)(2,1)S(1)}, bf16[2,1024,128]{2,1,0:T(8,128)(2,1)S(1)}, u32[]{:S(2)}, u32[]{:S(2)}) %collective-permute-start.2) | collective-permute-done | bytes 524320 | tf_op jit(solution)/shard_map/ppermute | solution.py:463
  38.6 0.0 copy-start.4
  38.6 7.2 %conv_run_0.1 = (bf16[3072,128]{1,0:T(8,128)(2,1)}, bf16[3072,128]{1,0:T(8,128)(2,1)}, bf16[256,3456]{1,0:T(8,128)(2,1)}) custom-call(bf16[3072,128]{1,0:T(8,128)(2,1)} %bitcast.12, bf16[3072,128]{1,0:T(8,128)(2,1)} %bitcast.19, s32[27,24,128]{2,1,0:T(8,128)} %bitcast.27, bf16[3456,128]{1,0:T(8,128)(2,1)} %bitcast.35, bf16[2,1024,128]{2,1,0:T(8,128)(2,1)} %copy-done.2), custom_call_target="tpu_custom_call" | custom-call | flops 1000000 | bytes 10000 | tf_op jit(solution)/shard_map/conv_run_0/pallas_call | solution.py:369
  45.9 0.0 all-to-all-done.refs_0_
  45.9 0.9 %sum_for_space.1 = bf16[4,432,128]{2,1,0:T(8,128)(2,1)} custom-call(bf16[4,432,128]{2,1,0:T(8,128)(2,1)S(1)} %all-to-all-done.refs_0_), custom_call_target="tpu_custom_call" | custom-call | flops 1000000 | bytes 10000 | tf_op jit(solution)/shard_map/sum_for_space/pallas_call | solution.py:410
  46.7 0.0 copy-done.4
  46.7 4.0 %all-to-all-start.1 = ((bf16[4,432,128]{2,1,0:T(8,128)(2,1)}), bf16[4,432,128]{2,1,0:T(8,128)(2,1)S(1)}, u32[]{:S(2)}, u32[]{:S(2)}) async-start(bf16[4,432,128]{2,1,0:T(8,128)(2,1)} %sum_for_space.1), calls=%async_computation.1 | async-start | bytes 884736 | tf_op jit(solution)/shard_map/all_to_all | solution.py:488
  50.7 11.3 %conv_run_1.1 = (bf16[3072,128]{1,0:T(8,128)(2,1)}, bf16[3072,128]{1,0:T(8,128)(2,1)}) custom-call(bf16[3072,128]{1,0:T(8,128)(2,1)} %bitcast.13, bf16[3072,128]{1,0:T(8,128)(2,1)} %bitcast.20, s32[27,24,128]{2,1,0:T(8,128)} %bitcast.28, bf16[256,3456]{1,0:T(8,128)(2,1)} %get-tuple-element.51.w_hbm, ...), custom_call_target="tpu_custom_call", output_to_operand_aliasing={{0}: (6, {}), {1}: (7, {})} | custom-call | flops 10000000000 | bytes 10000 | tf_op jit(solution)/shard_map/conv_run_1/pallas_call | solution.py:369
  62.1 1.3 %all-to-all-done.1.refs_0_ = bf16[4,432,128]{2,1,0:T(8,128)(2,1)S(1)} async-done(((bf16[4,432,128]{2,1,0:T(8,128)(2,1)}), bf16[4,432,128]{2,1,0:T(8,128)(2,1)S(1)}, u32[]{:S(2)}, u32[]{:S(2)}) %all-to-all-start.1) | async-done | bytes 442400 | tf_op jit(solution)/shard_map/all_to_all | solution.py:488
  63.3 0.8 %sum_for_dp.1 = bf16[4,432,128]{2,1,0:T(8,128)(2,1)} custom-call(bf16[4,432,128]{2,1,0:T(8,128)(2,1)S(1)} %all-to-all-done.1.refs_0_), custom_call_target="tpu_custom_call" | custom-call | flops 1000000 | bytes 10000 | tf_op jit(solution)/shard_map/sum_for_dp/pallas_call | solution.py:410
  64.2 3.7 %all-to-all-start.2 = ((bf16[4,432,128]{2,1,0:T(8,128)(2,1)}), bf16[4,432,128]{2,1,0:T(8,128)(2,1)S(1)}, u32[]{:S(2)}, u32[]{:S(2)}) async-start(bf16[4,432,128]{2,1,0:T(8,128)(2,1)} %sum_for_dp.1), calls=%async_computation.2 | async-start | bytes 884736 | tf_op jit(solution)/shard_map/all_to_all | solution.py:482
  67.9 6.9 %conv_run_2.1 = (bf16[3072,128]{1,0:T(8,128)(2,1)}, bf16[3072,128]{1,0:T(8,128)(2,1)}) custom-call(bf16[3072,128]{1,0:T(8,128)(2,1)} %bitcast.14, bf16[3072,128]{1,0:T(8,128)(2,1)} %bitcast.21, s32[27,24,128]{2,1,0:T(8,128)} %bitcast.29, bf16[256,3456]{1,0:T(8,128)(2,1)} %get-tuple-element.51.w_hbm, ...), custom_call_target="tpu_custom_call", output_to_operand_aliasing={{0}: (5, {}), {1}: (6, {})} | custom-call | flops 10000000000 | bytes 10000 | tf_op jit(solution)/shard_map/conv_run_2/pallas_call | solution.py:369
  74.8 0.0 all-to-all-done.2
  74.8 0.1 collective-permute-start.3
  74.9 1.0 %widen_own_half.1.rest_0_ = f32[3456,128]{1,0:T(8,128)} custom-call(bf16[1728,128]{1,0:T(8,128)(2,1)S(1)} %bitcast.26), custom_call_target="tpu_custom_call" | custom-call | tf_op jit(solution)/shard_map/widen_own_half/pallas_call | solution.py:434
  75.9 0.8 %collective-permute-done.3.in_ref = bf16[1728,128]{1,0:T(8,128)(2,1)S(1)} collective-permute-done((bf16[1728,128]{1,0:T(8,128)(2,1)S(1)}, bf16[1728,128]{1,0:T(8,128)(2,1)S(1)}, u32[]{:S(2)}, u32[]{:S(2)}) %collective-permute-start.3) | collective-permute-done | bytes 442400 | tf_op jit(solution)/shard_map/ppermute | solution.py:495
  76.7 0.9 %widen_other_half.1 = f32[3456,128]{1,0:T(8,128)} custom-call(bf16[1728,128]{1,0:T(8,128)(2,1)S(1)} %collective-permute-done.3.in_ref, f32[3456,128]{1,0:T(8,128)} %widen_own_half.1.rest_0_), custom_call_target="tpu_custom_call", output_to_operand_aliasing={{}: (1, {})} | custom-call | tf_op jit(solution)/shard_map/widen_other_half/pallas_call | solution.py:434
  (1 shorter events, 0.0 us)
Async XLA Ops:
  0.6 7.0 %copy-start.1 = (bf16[1,3072,128]{2,1,0:T(8,128)(2,1)S(1)}, bf16[1,3072,128]{2,1,0:T(8,128)(2,1)}, u32[]{:S(2)}) copy-start(bf16[1,3072,128]{2,1,0:T(8,128)(2,1)} %param.7) | copy-start | bytes 2359300
  0.6 7.0 %copy-start = (bf16[1,3072,128]{2,1,0:T(8,128)(2,1)S(1)}, bf16[1,3072,128]{2,1,0:T(8,128)(2,1)}, u32[]{:S(2)}) copy-start(bf16[1,3072,128]{2,1,0:T(8,128)(2,1)} %param.4) | copy-start | bytes 2359300
  0.7 7.0 %copy-start.3 = (s32[1,27,3072]{2,0,1:T(1,128)S(1)}, s32[1,27,3072]{2,0,1:T(1,128)}, u32[]{:S(2)}) copy-start(s32[1,27,3072]{2,0,1:T(1,128)} %param.5) | copy-start | bytes 995332
  2.7 16.4 %collective-permute-start = (bf16[2,1024,128]{2,1,0:T(8,128)(2,1)}, bf16[2,1024,128]{2,1,0:T(8,128)(2,1)S(1)}, u32[]{:S(2)}, u32[]{:S(2)}) collective-permute-start(bf16[2,1024,128]{2,1,0:T(8,128)(2,1)} %stack_last_layer.1), channel_id=1, source_target_pairs={{0,1},{1,2},{2,3},{4,5},{5,6},{6,7},{8,9},{9,10},{10,11},{12,13},{... | collective-permute-start | bytes 1572872 | tf_op jit(solution)/shard_map/ppermute | solution.py:454
  19.1 2.7 %copy-start.2 = (bf16[2,1024,128]{2,1,0:T(8,128)(2,1)}, bf16[2,1024,128]{2,1,0:T(8,128)(2,1)S(1)}, u32[]{:S(2)}) copy-start(bf16[2,1024,128]{2,1,0:T(8,128)(2,1)S(1)} %collective-permute-done.low_ref.rest_0_) | copy-start | bytes 1572868
  21.7 1.9 %collective-permute-start.1 = (bf16[1728,128]{1,0:T(8,128)(2,1)S(1)}, bf16[1728,128]{1,0:T(8,128)(2,1)S(1)}, u32[]{:S(2)}, u32[]{:S(2)}) collective-permute-start(bf16[1728,128]{1,0:T(8,128)(2,1)S(1)} %get-tuple-element.36), channel_id=1, source_target_pairs={{0,4},{4,0},{8,12},{12,8},{16,20},{20,16},{24,28},{28,24},{1,5},{5... | collective-permute-start | bytes 1327112 | tf_op jit(solution)/shard_map/ppermute | solution.py:468
  21.8 16.8 %collective-permute-start.2 = (bf16[2,1024,128]{2,1,0:T(8,128)(2,1)S(1)}, bf16[2,1024,128]{2,1,0:T(8,128)(2,1)S(1)}, u32[]{:S(2)}, u32[]{:S(2)}) collective-permute-start(bf16[2,1024,128]{2,1,0:T(8,128)(2,1)S(1)} %stack_first_layer.1), channel_id=1, source_target_pairs={{1,0},{2,1},{3,2},{5,4},{6,5},{7,6},{9,8},{10,9},{11,10},{13,12},{... | collective-permute-start | bytes 1572872 | tf_op jit(solution)/shard_map/ppermute | solution.py:463
  24.5 21.4 %all-to-all-start = ((bf16[4,432,128]{2,1,0:T(8,128)(2,1)}), bf16[4,432,128]{2,1,0:T(8,128)(2,1)S(1)}, u32[]{:S(2)}, u32[]{:S(2)}) async-start(bf16[4,432,128]{2,1,0:T(8,128)(2,1)} %bitcast.6), calls=%async_computation | async-start | bytes 884736 | tf_op jit(solution)/shard_map/all_to_all | solution.py:482
  38.6 8.1 %copy-start.4 = (bf16[2,1024,128]{2,1,0:T(8,128)(2,1)}, bf16[2,1024,128]{2,1,0:T(8,128)(2,1)S(1)}, u32[]{:S(2)}) copy-start(bf16[2,1024,128]{2,1,0:T(8,128)(2,1)S(1)} %collective-permute-done.2.rest_1_.rest_0_) | copy-start | bytes 1572868
  46.7 16.6 %all-to-all-start.1 = ((bf16[4,432,128]{2,1,0:T(8,128)(2,1)}), bf16[4,432,128]{2,1,0:T(8,128)(2,1)S(1)}, u32[]{:S(2)}, u32[]{:S(2)}) async-start(bf16[4,432,128]{2,1,0:T(8,128)(2,1)} %sum_for_space.1), calls=%async_computation.1 | async-start | bytes 884736 | tf_op jit(solution)/shard_map/all_to_all | solution.py:488
  64.2 10.7 %all-to-all-start.2 = ((bf16[4,432,128]{2,1,0:T(8,128)(2,1)}), bf16[4,432,128]{2,1,0:T(8,128)(2,1)S(1)}, u32[]{:S(2)}, u32[]{:S(2)}) async-start(bf16[4,432,128]{2,1,0:T(8,128)(2,1)} %sum_for_dp.1), calls=%async_computation.2 | async-start | bytes 884736 | tf_op jit(solution)/shard_map/all_to_all | solution.py:482
  74.8 1.9 %collective-permute-start.3 = (bf16[1728,128]{1,0:T(8,128)(2,1)S(1)}, bf16[1728,128]{1,0:T(8,128)(2,1)S(1)}, u32[]{:S(2)}, u32[]{:S(2)}) collective-permute-start(bf16[1728,128]{1,0:T(8,128)(2,1)S(1)} %bitcast.25), channel_id=1, source_target_pairs={{0,4},{4,0},{8,12},{12,8},{16,20},{20,16},{24,28},{28,24},{1,5},{5... | collective-permute-start | bytes 1327112 | tf_op jit(solution)/shard_map/ppermute | solution.py:495

commit v2 on v1

--- a/solution.py
+++ b/solution.py
@@ -454,15 +454,15 @@
     low = lax.ppermute(
         stack_layer(feats, grads, voxels // LAYER - 1, FULL_VMEM_LIMIT, "stack_last_layer"), "space", up
     )
+    high = lax.ppermute(
+        stack_layer(feats, grads, 0, VMEM_LIMIT, "stack_first_layer"), "space", down
+    )
 
     scale = 1.0 / math.sqrt(dp * space * voxels)
     share = -(-27 * channels // (16 * dp)) * 16
     inner = grad_w_inner(feats, grads, neigh)
-    inner, later_feats, later_grads = lax.optimization_barrier((inner, feats, grads))
-    first = stack_layer(later_feats, later_grads, 0, VMEM_LIMIT, "stack_first_layer")
-    high = lax.ppermute(first, "space", down)
-    inner, first = lax.optimization_barrier((inner, first))
     mine, other = grad_w_halo(feats, grads, low, neigh, inner, scale, share * dp)
+    mine, other, high = lax.optimization_barrier((mine, other, high))
     swap = [(i, i ^ 1) for i in range(dp)]
     alike = [list(range(0, dp, 2)), list(range(1, dp, 2))]
     other = lax.ppermute(other, "dp", swap)
@@ -482,7 +482,6 @@
         return lax.all_to_all(pieces, "dp", 0, 0, axis_index_groups=alike, tiled=True)
 
     pieces = exchange(mine.reshape(dp // 2, share, channels))
-    flat_weight, high = lax.optimization_barrier((flat_weight, high))
     done = conv((), 0)
     pieces, done = lax.optimization_barrier((pieces, done))
     pieces = lax.all_to_all(sum_parts((pieces,), space, "sum_for_space"), "space", 0, 0, tiled=True)

time: 78 us -> 69.4 us (0.89)
  waiting for transfers between devices: 16.4 us -> 7.52 us
    ppermute x1, waiting for transfers between devices: 10.4 us -> 1.23 us  [local(): lax.ppermute(stack_layer(feats, grads, 0, VMEM_LIMIT, 'stack_first_layer'...]
    ppermute x1, waiting for transfers between devices: 0.48 us -> 1.79 us  [local(): other = lax.ppermute(other, 'dp', swap)]
    ppermute x1, waiting for transfers between devices: 3.33 us -> 2.03 us  [local(): lax.ppermute(stack_layer(feats, grads, voxels // LAYER - 1, FULL_VMEM_LIM...]
  transfers between devices with their start and end apart: 7 -> 7, of which waited for: 5 -> 6; matrix products, arithmetic and copies ran while one was open for 0% -> 0% of each run, Pallas kernels for 46% -> 54%
where the time goes in v2:
time: 69.4 us; the launch traced here: 69 us
  Pallas kernels  42.5 us (61%)
  starting transfers between devices  18.3 us (26%)
  waiting for transfers between devices  7.52 us (11%)
  between operations  0.77 us (1%)
    pallas_call x3, Pallas kernels, conv_run(): pl.pallas_call(functools.partial(conv_kernel, voxels, run, len(halos), ma...  25.2 us
    pallas_call x1, Pallas kernels, grad_w_inner(): pl.pallas_call(functools.partial(weight_inner_kernel, voxels), out_shape=...  8.04 us
    all_to_all x2, starting transfers between devices, exchange(): lax.all_to_all(pieces, 'dp', 0, 0, axis_index_groups=alike, tiled=True)  7.42 us
    ppermute x1, starting transfers between devices, local(): lax.ppermute(stack_layer(feats, grads, voxels // LAYER - 1, FULL_VMEM_LIM...  4.95 us
    all_to_all x1, starting transfers between devices, local(): lax.all_to_all(sum_parts((pieces,), space, 'sum_for_space'), 'space', 0,...  4.52 us
    pallas_call x1, Pallas kernels, grad_w_halo(): pl.pallas_call(functools.partial(weight_halo_kernel, scale), out_shape=(o...  2.66 us
    pallas_call x3, Pallas kernels, sum_parts(): pl.pallas_call(sum_kernel, out_shape=jax.ShapeDtypeStruct((copies,) + sha...  2.58 us
    ppermute x1, waiting for transfers between devices, local(): lax.ppermute(stack_layer(feats, grads, voxels // LAYER - 1, FULL_VMEM_LIM...  2.03 us
  transfers between devices with their start and end apart: 7, of which 6 were waited for; matrix products, arithmetic and copies ran while one was open for 0% of the time, Pallas kernels for 54%

profile of v2, /device:TPU:0, one launch (start us, length us, event | category | flops | bytes accessed | tf_op | source)
XLA Modules:
  0.0 69.0 jit_solution(9843935095463897395)
XLA Ops:
  0.6 0.0 copy-start.1
  0.6 0.0 copy-start
  0.7 0.0 copy-start.3
  0.7 2.0 %stack_last_layer.1 = bf16[2,1024,128]{2,1,0:T(8,128)(2,1)} custom-call(bf16[3072,128]{1,0:T(8,128)(2,1)} %bitcast.11, bf16[3072,128]{1,0:T(8,128)(2,1)} %bitcast.18), custom_call_target="tpu_custom_call" | custom-call | tf_op jit(solution)/shard_map/stack_last_layer/pallas_call | solution.py:228
  2.7 4.9 %collective-permute-start = (bf16[2,1024,128]{2,1,0:T(8,128)(2,1)}, bf16[2,1024,128]{2,1,0:T(8,128)(2,1)S(1)}, u32[]{:S(2)}, u32[]{:S(2)}) collective-permute-start(bf16[2,1024,128]{2,1,0:T(8,128)(2,1)} %stack_last_layer.1), channel_id=1, source_target_pairs={{0,1},{1,2},{2,3},{4,5},{5,6},{6,7},{8,9},{9,10},{10,11},{12,13},{... | collective-permute-start | bytes 1572872 | tf_op jit(solution)/shard_map/ppermute | solution.py:454
  7.6 0.0 copy-done.1
  7.6 0.0 copy-done
  7.7 1.3 %collective-permute-start.1 = (bf16[2,1024,128]{2,1,0:T(8,128)(2,1)S(1)}, bf16[2,1024,128]{2,1,0:T(8,128)(2,1)S(1)}, u32[]{:S(2)}, u32[]{:S(2)}) collective-permute-start(bf16[2,1024,128]{2,1,0:T(8,128)(2,1)S(1)} %stack_first_layer.1), channel_id=1, source_target_pairs={{1,0},{2,1},{3,2},{5,4},{6,5},{7,6},{9,8},{10,9},{11,10},{13,12},{... | collective-permute-start | bytes 1572872 | tf_op jit(solution)/shard_map/ppermute | solution.py:457
  9.0 0.0 copy-done.3
  9.0 8.0 %weight_gradient_inner.1.in_ref = f32[128,3456]{1,0:T(8,128)S(1)} custom-call(bf16[3072,128]{1,0:T(8,128)(2,1)S(1)} %bitcast.16, bf16[3072,128]{1,0:T(8,128)(2,1)S(1)} %bitcast.23, s32[27,24,128]{2,1,0:T(8,128)S(1)} %bitcast.30), custom_call_target="tpu_custom_call" | custom-call | flops 8000000000 | bytes 4000000 | tf_op jit(solution)/shard_map/weight_gradient_inner/pallas_call | solution.py:189
  17.0 2.0 %collective-permute-done.low_ref.rest_0_ = bf16[2,1024,128]{2,1,0:T(8,128)(2,1)S(1)} collective-permute-done((bf16[2,1024,128]{2,1,0:T(8,128)(2,1)}, bf16[2,1024,128]{2,1,0:T(8,128)(2,1)S(1)}, u32[]{:S(2)}, u32[]{:S(2)}) %collective-permute-start) | collective-permute-done | bytes 524320 | tf_op jit(solution)/shard_map/ppermute | solution.py:454
  19.1 0.0 copy-start.2
  19.1 2.7 %weight_gradient_halo.1 = (bf16[1728,128]{1,0:T(8,128)(2,1)S(1)}, bf16[1728,128]{1,0:T(8,128)(2,1)S(1)}) custom-call(bf16[3072,128]{1,0:T(8,128)(2,1)S(1)} %bitcast.17, bf16[3072,128]{1,0:T(8,128)(2,1)S(1)} %bitcast.24, bf16[2,1024,128]{2,1,0:T(8,128)(2,1)S(1)} %collective-permute-done.low_ref.rest_0_, s32[27,24,128]{2,1,0:T(8,128)S(1)} %bitcast.31, ...), custom_call_target="tpu_custom_call" | custom-call | flops 1000000 | bytes 10000 | tf_op jit(solution)/shard_map/weight_gradient_halo/pallas_call | solution.py:204
  21.7 0.0 copy-done.2
  21.7 1.2 %collective-permute-done.1.rest_1_.rest_0_ = bf16[2,1024,128]{2,1,0:T(8,128)(2,1)S(1)} collective-permute-done((bf16[2,1024,128]{2,1,0:T(8,128)(2,1)S(1)}, bf16[2,1024,128]{2,1,0:T(8,128)(2,1)S(1)}, u32[]{:S(2)}, u32[]{:S(2)}) %collective-permute-start.1) | collective-permute-done | bytes 524320 | tf_op jit(solution)/shard_map/ppermute | solution.py:457
  23.0 0.0 copy-start.4
  23.0 0.0 collective-permute-start.2
  23.0 1.8 %collective-permute-done.2 = bf16[1728,128]{1,0:T(8,128)(2,1)S(1)} collective-permute-done((bf16[1728,128]{1,0:T(8,128)(2,1)S(1)}, bf16[1728,128]{1,0:T(8,128)(2,1)S(1)}, u32[]{:S(2)}, u32[]{:S(2)}) %collective-permute-start.2) | collective-permute-done | bytes 442400 | tf_op jit(solution)/shard_map/ppermute | solution.py:468
  24.7 0.9 %sum_of_pair.1 = bf16[1,1728,128]{2,1,0:T(8,128)(2,1)} custom-call(bf16[1,1728,128]{2,1,0:T(8,128)(2,1)S(1)} %bitcast.32, bf16[1,1728,128]{2,1,0:T(8,128)(2,1)S(1)} %bitcast.33), custom_call_target="tpu_custom_call" | custom-call | flops 1000000 | bytes 10000 | tf_op jit(solution)/shard_map/sum_of_pair/pallas_call | solution.py:410
  25.6 3.7 %all-to-all-start = ((bf16[4,432,128]{2,1,0:T(8,128)(2,1)}), bf16[4,432,128]{2,1,0:T(8,128)(2,1)S(1)}, u32[]{:S(2)}, u32[]{:S(2)}) async-start(bf16[4,432,128]{2,1,0:T(8,128)(2,1)} %bitcast.6), calls=%async_computation | async-start | bytes 884736 | tf_op jit(solution)/shard_map/all_to_all | solution.py:482
  29.4 7.0 %conv_run_0.1 = (bf16[3072,128]{1,0:T(8,128)(2,1)}, bf16[3072,128]{1,0:T(8,128)(2,1)}, bf16[256,3456]{1,0:T(8,128)(2,1)}) custom-call(bf16[3072,128]{1,0:T(8,128)(2,1)} %bitcast.12, bf16[3072,128]{1,0:T(8,128)(2,1)} %bitcast.19, s32[27,24,128]{2,1,0:T(8,128)} %bitcast.27, bf16[3456,128]{1,0:T(8,128)(2,1)} %bitcast.35, bf16[2,1024,128]{2,1,0:T(8,128)(2,1)} %copy-done.2), custom_call_target="tpu_custom_call" | custom-call | flops 1000000 | bytes 10000 | tf_op jit(solution)/shard_map/conv_run_0/pallas_call | solution.py:369
  36.4 0.0 copy-done.4
  36.4 0.4 all-to-all-done.refs_0_
  36.8 0.9 %sum_for_space.1 = bf16[4,432,128]{2,1,0:T(8,128)(2,1)} custom-call(bf16[4,432,128]{2,1,0:T(8,128)(2,1)S(1)} %all-to-all-done.refs_0_), custom_call_target="tpu_custom_call" | custom-call | flops 1000000 | bytes 10000 | tf_op jit(solution)/shard_map/sum_for_space/pallas_call | solution.py:410
  37.7 4.5 %all-to-all-start.1 = ((bf16[4,432,128]{2,1,0:T(8,128)(2,1)}), bf16[4,432,128]{2,1,0:T(8,128)(2,1)S(1)}, u32[]{:S(2)}, u32[]{:S(2)}) async-start(bf16[4,432,128]{2,1,0:T(8,128)(2,1)} %sum_for_space.1), calls=%async_computation.1 | async-start | bytes 884736 | tf_op jit(solution)/shard_map/all_to_all | solution.py:487
  42.2 11.3 %conv_run_1.1 = (bf16[3072,128]{1,0:T(8,128)(2,1)}, bf16[3072,128]{1,0:T(8,128)(2,1)}) custom-call(bf16[3072,128]{1,0:T(8,128)(2,1)} %bitcast.13, bf16[3072,128]{1,0:T(8,128)(2,1)} %bitcast.20, s32[27,24,128]{2,1,0:T(8,128)} %bitcast.28, bf16[256,3456]{1,0:T(8,128)(2,1)} %get-tuple-element.45.w_hbm, ...), custom_call_target="tpu_custom_call", output_to_operand_aliasing={{0}: (6, {}), {1}: (7, {})} | custom-call | flops 10000000000 | bytes 10000 | tf_op jit(solution)/shard_map/conv_run_1/pallas_call | solution.py:369
  53.5 1.3 %all-to-all-done.1.refs_0_ = bf16[4,432,128]{2,1,0:T(8,128)(2,1)S(1)} async-done(((bf16[4,432,128]{2,1,0:T(8,128)(2,1)}), bf16[4,432,128]{2,1,0:T(8,128)(2,1)S(1)}, u32[]{:S(2)}, u32[]{:S(2)}) %all-to-all-start.1) | async-done | bytes 442400 | tf_op jit(solution)/shard_map/all_to_all | solution.py:487
  54.8 0.8 %sum_for_dp.1 = bf16[4,432,128]{2,1,0:T(8,128)(2,1)} custom-call(bf16[4,432,128]{2,1,0:T(8,128)(2,1)S(1)} %all-to-all-done.1.refs_0_), custom_call_target="tpu_custom_call" | custom-call | flops 1000000 | bytes 10000 | tf_op jit(solution)/shard_map/sum_for_dp/pallas_call | solution.py:410
  55.6 3.7 %all-to-all-start.2 = ((bf16[4,432,128]{2,1,0:T(8,128)(2,1)}), bf16[4,432,128]{2,1,0:T(8,128)(2,1)S(1)}, u32[]{:S(2)}, u32[]{:S(2)}) async-start(bf16[4,432,128]{2,1,0:T(8,128)(2,1)} %sum_for_dp.1), calls=%async_computation.2 | async-start | bytes 884736 | tf_op jit(solution)/shard_map/all_to_all | solution.py:482
  59.3 6.9 %conv_run_2.1 = (bf16[3072,128]{1,0:T(8,128)(2,1)}, bf16[3072,128]{1,0:T(8,128)(2,1)}) custom-call(bf16[3072,128]{1,0:T(8,128)(2,1)} %bitcast.14, bf16[3072,128]{1,0:T(8,128)(2,1)} %bitcast.21, s32[27,24,128]{2,1,0:T(8,128)} %bitcast.29, bf16[256,3456]{1,0:T(8,128)(2,1)} %get-tuple-element.45.w_hbm, ...), custom_call_target="tpu_custom_call", output_to_operand_aliasing={{0}: (5, {}), {1}: (6, {})} | custom-call | flops 10000000000 | bytes 10000 | tf_op jit(solution)/shard_map/conv_run_2/pallas_call | solution.py:369
  66.2 0.0 all-to-all-done.2
  66.2 0.1 collective-permute-start.3
  66.3 1.0 %widen_own_half.1.rest_0_ = f32[3456,128]{1,0:T(8,128)} custom-call(bf16[1728,128]{1,0:T(8,128)(2,1)S(1)} %bitcast.26), custom_call_target="tpu_custom_call" | custom-call | tf_op jit(solution)/shard_map/widen_own_half/pallas_call | solution.py:434
  67.3 0.8 %collective-permute-done.3.in_ref = bf16[1728,128]{1,0:T(8,128)(2,1)S(1)} collective-permute-done((bf16[1728,128]{1,0:T(8,128)(2,1)S(1)}, bf16[1728,128]{1,0:T(8,128)(2,1)S(1)}, u32[]{:S(2)}, u32[]{:S(2)}) %collective-permute-start.3) | collective-permute-done | bytes 442400 | tf_op jit(solution)/shard_map/ppermute | solution.py:494
  68.1 0.9 %widen_other_half.1 = f32[3456,128]{1,0:T(8,128)} custom-call(bf16[1728,128]{1,0:T(8,128)(2,1)S(1)} %collective-permute-done.3.in_ref, f32[3456,128]{1,0:T(8,128)} %widen_own_half.1.rest_0_), custom_call_target="tpu_custom_call", output_to_operand_aliasing={{}: (1, {})} | custom-call | tf_op jit(solution)/shard_map/widen_other_half/pallas_call | solution.py:434
  (1 shorter events, 0.0 us)
Async XLA Ops:
  0.6 7.0 %copy-start.1 = (bf16[1,3072,128]{2,1,0:T(8,128)(2,1)S(1)}, bf16[1,3072,128]{2,1,0:T(8,128)(2,1)}, u32[]{:S(2)}) copy-start(bf16[1,3072,128]{2,1,0:T(8,128)(2,1)} %param.7) | copy-start | bytes 2359300
  0.6 7.0 %copy-start = (bf16[1,3072,128]{2,1,0:T(8,128)(2,1)S(1)}, bf16[1,3072,128]{2,1,0:T(8,128)(2,1)}, u32[]{:S(2)}) copy-start(bf16[1,3072,128]{2,1,0:T(8,128)(2,1)} %param.4) | copy-start | bytes 2359300
  0.7 8.3 %copy-start.3 = (s32[1,27,3072]{2,0,1:T(1,128)S(1)}, s32[1,27,3072]{2,0,1:T(1,128)}, u32[]{:S(2)}) copy-start(s32[1,27,3072]{2,0,1:T(1,128)} %param.5) | copy-start | bytes 995332
  2.7 16.4 %collective-permute-start = (bf16[2,1024,128]{2,1,0:T(8,128)(2,1)}, bf16[2,1024,128]{2,1,0:T(8,128)(2,1)S(1)}, u32[]{:S(2)}, u32[]{:S(2)}) collective-permute-start(bf16[2,1024,128]{2,1,0:T(8,128)(2,1)} %stack_last_layer.1), channel_id=1, source_target_pairs={{0,1},{1,2},{2,3},{4,5},{5,6},{6,7},{8,9},{9,10},{10,11},{12,13},{... | collective-permute-start | bytes 1572872 | tf_op jit(solution)/shard_map/ppermute | solution.py:454
  7.7 15.3 %collective-permute-start.1 = (bf16[2,1024,128]{2,1,0:T(8,128)(2,1)S(1)}, bf16[2,1024,128]{2,1,0:T(8,128)(2,1)S(1)}, u32[]{:S(2)}, u32[]{:S(2)}) collective-permute-start(bf16[2,1024,128]{2,1,0:T(8,128)(2,1)S(1)} %stack_first_layer.1), channel_id=1, source_target_pairs={{1,0},{2,1},{3,2},{5,4},{6,5},{7,6},{9,8},{10,9},{11,10},{13,12},{... | collective-permute-start | bytes 1572872 | tf_op jit(solution)/shard_map/ppermute | solution.py:457
  19.1 2.7 %copy-start.2 = (bf16[2,1024,128]{2,1,0:T(8,128)(2,1)}, bf16[2,1024,128]{2,1,0:T(8,128)(2,1)S(1)}, u32[]{:S(2)}) copy-start(bf16[2,1024,128]{2,1,0:T(8,128)(2,1)S(1)} %collective-permute-done.low_ref.rest_0_) | copy-start | bytes 1572868
  23.0 13.4 %copy-start.4 = (bf16[2,1024,128]{2,1,0:T(8,128)(2,1)}, bf16[2,1024,128]{2,1,0:T(8,128)(2,1)S(1)}, u32[]{:S(2)}) copy-start(bf16[2,1024,128]{2,1,0:T(8,128)(2,1)S(1)} %collective-permute-done.1.rest_1_.rest_0_) | copy-start | bytes 1572868
  23.0 1.8 %collective-permute-start.2 = (bf16[1728,128]{1,0:T(8,128)(2,1)S(1)}, bf16[1728,128]{1,0:T(8,128)(2,1)S(1)}, u32[]{:S(2)}, u32[]{:S(2)}) collective-permute-start(bf16[1728,128]{1,0:T(8,128)(2,1)S(1)} %get-tuple-element.31), channel_id=1, source_target_pairs={{0,4},{4,0},{8,12},{12,8},{16,20},{20,16},{24,28},{28,24},{1,5},{5... | collective-permute-start | bytes 1327112 | tf_op jit(solution)/shard_map/ppermute | solution.py:468
  25.6 11.2 %all-to-all-start = ((bf16[4,432,128]{2,1,0:T(8,128)(2,1)}), bf16[4,432,128]{2,1,0:T(8,128)(2,1)S(1)}, u32[]{:S(2)}, u32[]{:S(2)}) async-start(bf16[4,432,128]{2,1,0:T(8,128)(2,1)} %bitcast.6), calls=%async_computation | async-start | bytes 884736 | tf_op jit(solution)/shard_map/all_to_all | solution.py:482
  37.7 17.1 %all-to-all-start.1 = ((bf16[4,432,128]{2,1,0:T(8,128)(2,1)}), bf16[4,432,128]{2,1,0:T(8,128)(2,1)S(1)}, u32[]{:S(2)}, u32[]{:S(2)}) async-start(bf16[4,432,128]{2,1,0:T(8,128)(2,1)} %sum_for_space.1), calls=%async_computation.1 | async-start | bytes 884736 | tf_op jit(solution)/shard_map/all_to_all | solution.py:487
  55.6 10.6 %all-to-all-start.2 = ((bf16[4,432,128]{2,1,0:T(8,128)(2,1)}), bf16[4,432,128]{2,1,0:T(8,128)(2,1)S(1)}, u32[]{:S(2)}, u32[]{:S(2)}) async-start(bf16[4,432,128]{2,1,0:T(8,128)(2,1)} %sum_for_dp.1), calls=%async_computation.2 | async-start | bytes 884736 | tf_op jit(solution)/shard_map/all_to_all | solution.py:482
  66.2 1.9 %collective-permute-start.3 = (bf16[1728,128]{1,0:T(8,128)(2,1)S(1)}, bf16[1728,128]{1,0:T(8,128)(2,1)S(1)}, u32[]{:S(2)}, u32[]{:S(2)}) collective-permute-start(bf16[1728,128]{1,0:T(8,128)(2,1)S(1)} %bitcast.25), channel_id=1, source_target_pairs={{0,4},{4,0},{8,12},{12,8},{16,20},{20,16},{24,28},{28,24},{1,5},{5... | collective-permute-start | bytes 1327112 | tf_op jit(solution)/shard_map/ppermute | solution.py:494

commit v3 on v2

--- a/solution.py
+++ b/solution.py
@@ -222,7 +222,26 @@
     out_ref[1] = g_ref[...]
 
 
-def stack_layer(feats, grads, layer, vmem, name):
+def stack_by_copies_kernel(layer, f_ref, g_ref, out_ref, held, sems):
+    rows = pl.ds(layer * LAYER, LAYER)
+    copies = []
+    for i, ref in enumerate((f_ref, g_ref)):
+        copies.append(
+            (
+                pltpu.make_async_copy(ref.at[rows, :], held.at[i], sems.at[i]),
+                pltpu.make_async_copy(held.at[i], out_ref.at[i], sems.at[2 + i]),
+            )
+        )
+    for fetch, _ in copies:
+        fetch.start()
+    for fetch, store in copies:
+        fetch.wait()
+        store.start()
+    for _, store in copies:
+        store.wait()
+
+
+def stack_layer(feats, grads, layer, name):
     channels = feats.shape[1]
     block = pl.BlockSpec((LAYER, channels), lambda i: (layer, 0))
     return pl.pallas_call(
@@ -231,7 +250,21 @@
         out_shape=jax.ShapeDtypeStruct((2, LAYER, channels), jnp.bfloat16),
         in_specs=[block, block],
         out_specs=VMEM,
-        compiler_params=pltpu.CompilerParams(vmem_limit_bytes=vmem),
+        compiler_params=pltpu.CompilerParams(vmem_limit_bytes=VMEM_LIMIT),
+        name=name,
+    )(feats, grads)
+
+
+def stack_layer_by_copies(feats, grads, layer, name):
+    channels = feats.shape[1]
+    shape = (2, LAYER, channels)
+    return pl.pallas_call(
+        functools.partial(stack_by_copies_kernel, layer),
+        out_shape=jax.ShapeDtypeStruct(shape, jnp.bfloat16),
+        in_specs=[HBM, HBM],
+        out_specs=HBM,
+        scratch_shapes=[pltpu.VMEM(shape, jnp.bfloat16), pltpu.SemaphoreType.DMA((4,))],
+        compiler_params=pltpu.CompilerParams(vmem_limit_bytes=FULL_VMEM_LIMIT),
         name=name,
     )(feats, grads)
 
@@ -452,26 +485,29 @@
     up = [(i, i + 1) for i in range(space - 1)]
     down = [(i + 1, i) for i in range(space - 1)]
     low = lax.ppermute(
-        stack_layer(feats, grads, voxels // LAYER - 1, FULL_VMEM_LIMIT, "stack_last_layer"), "space", up
+        stack_layer_by_copies(feats, grads, voxels // LAYER - 1, "stack_last_layer"), "space", up
     )
     high = lax.ppermute(
-        stack_layer(feats, grads, 0, VMEM_LIMIT, "stack_first_layer"), "space", down
+        stack_layer(feats, grads, 0, "stack_first_layer"), "space", down
     )
 
     scale = 1.0 / math.sqrt(dp * space * voxels)
-    share = -(-27 * channels // (16 * dp)) * 16
+    group = dp // 2 * space
+    share = -(-27 * channels // (32 * group)) * 16
+    swap = [(i, i ^ 1) for i in range(dp)]
+    alike = [
+        [d * space + z for d in range(side, dp, 2) for z in range(space)] for side in range(2)
+    ]
     inner = grad_w_inner(feats, grads, neigh)
-    mine, other = grad_w_halo(feats, grads, low, neigh, inner, scale, share * dp)
+    mine, other = grad_w_halo(feats, grads, low, neigh, inner, scale, 2 * group * share)
     mine, other, high = lax.optimization_barrier((mine, other, high))
-    swap = [(i, i ^ 1) for i in range(dp)]
-    alike = [list(range(0, dp, 2)), list(range(1, dp, 2))]
     other = lax.ppermute(other, "dp", swap)
     mine = sum_parts((mine[None], other[None]), 1, "sum_of_pair")
     mine, flat_weight = lax.optimization_barrier(
         (mine, weight.reshape(27 * channels, channels))
     )
-    chunks = voxels // CHUNK_C
-    ends = [0, chunks // 4 * CHUNK_C, chunks * 3 // 4 * CHUNK_C, voxels]
+    half = voxels // CHUNK_C // 2 * CHUNK_C
+    ends = [0, half, voxels]
 
     def conv(done, part):
         run = (ends[part], ends[part + 1])
@@ -479,18 +515,17 @@
         return conv_run(feats, grads, low, high, neigh, flat_weight, run, done, name)
 
     def exchange(pieces):
-        return lax.all_to_all(pieces, "dp", 0, 0, axis_index_groups=alike, tiled=True)
-
-    pieces = exchange(mine.reshape(dp // 2, share, channels))
+        return lax.all_to_all(
+            pieces, ("dp", "space"), 0, 0, axis_index_groups=alike, tiled=True
+        )
+
+    pieces = exchange(mine.reshape(group, share, channels))
     done = conv((), 0)
     pieces, done = lax.optimization_barrier((pieces, done))
-    pieces = lax.all_to_all(sum_parts((pieces,), space, "sum_for_space"), "space", 0, 0, tiled=True)
+    pieces = exchange(sum_parts((pieces,), group, "sum_and_spread"))
     done = conv(done, 1)
     pieces, done = lax.optimization_barrier((pieces, done))
-    pieces = exchange(sum_parts((pieces,), dp // 2, "sum_for_dp"))
-    done = conv(done, 2)
-    pieces, done = lax.optimization_barrier((pieces, done))
-    mine = pieces.reshape(dp // 2 * share, channels)
+    mine = pieces.reshape(group * share, channels)
     other = lax.ppermute(mine, "dp", swap)
     grad_w = widen(mine, True, 27 * channels, (), "widen_own_half")
     grad_w = widen(other, False, 27 * channels, (grad_w,), "widen_other_half")

time: 69.4 us -> 69.1 us (level)
  waiting for transfers between devices: 7.52 us -> 12.3 us
  Pallas kernels: 42.5 us -> 39 us
  starting transfers between devices: 18.3 us -> 16.6 us
    all_to_all x3 -> x2, waiting for transfers between devices: 1.67 us -> 6.32 us  [exchange(): lax.all_to_all(pieces, ('dp', 'space'), 0, 0, axis_index_groups=alike, ti...]
    pallas_call x3 -> x2, Pallas kernels: 25.2 us -> 22.8 us  [conv_run(): pl.pallas_call(functools.partial(conv_kernel, voxels, run, len(halos), ma...]
    pallas_call x2 -> x1, Pallas kernels: 2.03 us -> 0.04 us  [stack_layer(): pl.pallas_call(stack_kernel, grid=(1,), out_shape=jax.ShapeDtypeStruct((2...]
    pallas_call x0 -> x1, Pallas kernels: none -> 1.91 us  [stack_layer_by_copies(): pl.pallas_call(functools.partial(stack_by_copies_kernel, layer), out_shap...]
    all_to_all x3 -> x2, starting transfers between devices: 11.9 us -> 10.3 us  [exchange(): lax.all_to_all(pieces, ('dp', 'space'), 0, 0, axis_index_groups=alike, ti...]
    pallas_call x3 -> x2, Pallas kernels: 2.58 us -> 1.73 us  [sum_parts(): pl.pallas_call(sum_kernel, out_shape=jax.ShapeDtypeStruct((copies,) + sha...]
  transfers between devices with their start and end apart: 7 -> 6, of which waited for: 6 -> 6; matrix products, arithmetic and copies ran while one was open for 0% -> 0% of each run, Pallas kernels for 54% -> 50%
where the time goes in v3:
time: 69.1 us; the launch traced here: 68.6 us
  Pallas kernels  39 us (56%)
  starting transfers between devices  16.6 us (24%)
  waiting for transfers between devices  12.3 us (18%)
  between operations  0.76 us (1%)
    pallas_call x2, Pallas kernels, conv_run(): pl.pallas_call(functools.partial(conv_kernel, voxels, run, len(halos), ma...  22.8 us
    all_to_all x2, starting transfers between devices, exchange(): lax.all_to_all(pieces, ('dp', 'space'), 0, 0, axis_index_groups=alike, ti...  10.3 us
    pallas_call x1, Pallas kernels, grad_w_inner(): pl.pallas_call(functools.partial(weight_inner_kernel, voxels), out_shape=...  8.04 us
    all_to_all x2, waiting for transfers between devices, exchange(): lax.all_to_all(pieces, ('dp', 'space'), 0, 0, axis_index_groups=alike, ti...  6.32 us
    ppermute x1, starting transfers between devices, local(): lax.ppermute(stack_layer_by_copies(feats, grads, voxels // LAYER - 1, 'st...  4.96 us
    pallas_call x1, Pallas kernels, grad_w_halo(): pl.pallas_call(functools.partial(weight_halo_kernel, scale), out_shape=(o...  2.66 us
    ppermute x1, waiting for transfers between devices, local(): lax.ppermute(stack_layer_by_copies(feats, grads, voxels // LAYER - 1, 'st...  2.03 us
    pallas_call x1, Pallas kernels, stack_layer_by_copies(): pl.pallas_call(functools.partial(stack_by_copies_kernel, layer), out_shap...  1.91 us
  transfers between devices with their start and end apart: 6, of which 6 were waited for; matrix products, arithmetic and copies ran while one was open for 0% of the time, Pallas kernels for 50%

profile of v3, /device:TPU:0, one launch (start us, length us, event | category | flops | bytes accessed | tf_op | source)
XLA Modules:
  0.0 68.6 jit_solution(9874274647841623605)
XLA Ops:
  0.6 0.0 copy-start.1
  0.6 0.0 copy-start
  0.7 0.0 copy-start.3
  0.7 1.9 %stack_last_layer.1 = bf16[2,1024,128]{2,1,0:T(8,128)(2,1)} custom-call(bf16[3072,128]{1,0:T(8,128)(2,1)} %bitcast.11, bf16[3072,128]{1,0:T(8,128)(2,1)} %bitcast.17), custom_call_target="tpu_custom_call" | custom-call | tf_op jit(solution)/shard_map/stack_last_layer/pallas_call | solution.py:261
  2.6 5.0 %collective-permute-start = (bf16[2,1024,128]{2,1,0:T(8,128)(2,1)}, bf16[2,1024,128]{2,1,0:T(8,128)(2,1)S(1)}, u32[]{:S(2)}, u32[]{:S(2)}) collective-permute-start(bf16[2,1024,128]{2,1,0:T(8,128)(2,1)} %stack_last_layer.1), channel_id=1, source_target_pairs={{0,1},{1,2},{2,3},{4,5},{5,6},{6,7},{8,9},{9,10},{10,11},{12,13},{... | collective-permute-start | bytes 1572872 | tf_op jit(solution)/shard_map/ppermute | solution.py:487
  7.5 0.0 copy-done.1
  7.6 0.0 copy-done
  7.6 1.3 %collective-permute-start.1 = (bf16[2,1024,128]{2,1,0:T(8,128)(2,1)S(1)}, bf16[2,1024,128]{2,1,0:T(8,128)(2,1)S(1)}, u32[]{:S(2)}, u32[]{:S(2)}) collective-permute-start(bf16[2,1024,128]{2,1,0:T(8,128)(2,1)S(1)} %stack_first_layer.1), channel_id=1, source_target_pairs={{1,0},{2,1},{3,2},{5,4},{6,5},{7,6},{9,8},{10,9},{11,10},{13,12},{... | collective-permute-start | bytes 1572872 | tf_op jit(solution)/shard_map/ppermute | solution.py:490
  8.9 0.0 copy-done.3
  8.9 8.0 %weight_gradient_inner.1.in_ref = f32[128,3456]{1,0:T(8,128)S(1)} custom-call(bf16[3072,128]{1,0:T(8,128)(2,1)S(1)} %bitcast.15, bf16[3072,128]{1,0:T(8,128)(2,1)S(1)} %bitcast.21, s32[27,24,128]{2,1,0:T(8,128)S(1)} %bitcast.27), custom_call_target="tpu_custom_call" | custom-call | flops 8000000000 | bytes 4000000 | tf_op jit(solution)/shard_map/weight_gradient_inner/pallas_call | solution.py:189
  17.0 2.0 %collective-permute-done.low_ref.rest_0_ = bf16[2,1024,128]{2,1,0:T(8,128)(2,1)S(1)} collective-permute-done((bf16[2,1024,128]{2,1,0:T(8,128)(2,1)}, bf16[2,1024,128]{2,1,0:T(8,128)(2,1)S(1)}, u32[]{:S(2)}, u32[]{:S(2)}) %collective-permute-start) | collective-permute-done | bytes 524320 | tf_op jit(solution)/shard_map/ppermute | solution.py:487
  19.0 0.0 copy-start.2
  19.0 2.7 %weight_gradient_halo.1 = (bf16[1792,128]{1,0:T(8,128)(2,1)S(1)}, bf16[1792,128]{1,0:T(8,128)(2,1)S(1)}) custom-call(bf16[3072,128]{1,0:T(8,128)(2,1)S(1)} %bitcast.16, bf16[3072,128]{1,0:T(8,128)(2,1)S(1)} %bitcast.22, bf16[2,1024,128]{2,1,0:T(8,128)(2,1)S(1)} %collective-permute-done.low_ref.rest_0_, s32[27,24,128]{2,1,0:T(8,128)S(1)} %bitcast.28, ...), custom_call_target="tpu_custom_call" | custom-call | flops 1000000 | bytes 10000 | tf_op jit(solution)/shard_map/weight_gradient_halo/pallas_call | solution.py:204
  21.7 0.0 copy-done.2
  21.7 1.2 %collective-permute-done.1.rest_0_ = bf16[2,1024,128]{2,1,0:T(8,128)(2,1)S(1)} collective-permute-done((bf16[2,1024,128]{2,1,0:T(8,128)(2,1)S(1)}, bf16[2,1024,128]{2,1,0:T(8,128)(2,1)S(1)}, u32[]{:S(2)}, u32[]{:S(2)}) %collective-permute-start.1) | collective-permute-done | bytes 524320 | tf_op jit(solution)/shard_map/ppermute | solution.py:490
  22.9 0.0 copy-start.4
  22.9 0.0 collective-permute-start.2
  22.9 1.8 %collective-permute-done.2 = bf16[1792,128]{1,0:T(8,128)(2,1)S(1)} collective-permute-done((bf16[1792,128]{1,0:T(8,128)(2,1)S(1)}, bf16[1792,128]{1,0:T(8,128)(2,1)S(1)}, u32[]{:S(2)}, u32[]{:S(2)}) %collective-permute-start.2) | collective-permute-done | bytes 458784 | tf_op jit(solution)/shard_map/ppermute | solution.py:504
  24.7 0.9 %sum_of_pair.1 = bf16[1,1792,128]{2,1,0:T(8,128)(2,1)} custom-call(bf16[1,1792,128]{2,1,0:T(8,128)(2,1)S(1)} %bitcast.29, bf16[1,1792,128]{2,1,0:T(8,128)(2,1)S(1)} %bitcast.30), custom_call_target="tpu_custom_call" | custom-call | flops 1000000 | bytes 10000 | tf_op jit(solution)/shard_map/sum_of_pair/pallas_call | solution.py:443
  25.6 6.5 %all-to-all-start = ((bf16[16,112,128]{2,1,0:T(8,128)(2,1)}), bf16[16,112,128]{2,1,0:T(8,128)(2,1)S(1)}, u32[]{:S(2)}, u32[]{:S(2)}) async-start(bf16[16,112,128]{2,1,0:T(8,128)(2,1)} %bitcast.6), calls=%async_computation | async-start | bytes 917504 | tf_op jit(solution)/shard_map/all_to_all | solution.py:518
  32.1 11.5 %conv_run_0.1 = (bf16[3072,128]{1,0:T(8,128)(2,1)}, bf16[3072,128]{1,0:T(8,128)(2,1)}, bf16[256,3456]{1,0:T(8,128)(2,1)}) custom-call(bf16[3072,128]{1,0:T(8,128)(2,1)} %bitcast.12, bf16[3072,128]{1,0:T(8,128)(2,1)} %bitcast.18, s32[27,24,128]{2,1,0:T(8,128)} %bitcast.25, bf16[3456,128]{1,0:T(8,128)(2,1)} %bitcast.32, bf16[2,1024,128]{2,1,0:T(8,128)(2,1)} %copy-done.2), custom_call_target="tpu_custom_call" | custom-call | flops 1000000 | bytes 10000 | tf_op jit(solution)/shard_map/conv_run_0/pallas_call | solution.py:402
  43.6 0.0 copy-done.4
  43.6 3.6 %all-to-all-done.refs_0_ = bf16[16,112,128]{2,1,0:T(8,128)(2,1)S(1)} async-done(((bf16[16,112,128]{2,1,0:T(8,128)(2,1)}), bf16[16,112,128]{2,1,0:T(8,128)(2,1)S(1)}, u32[]{:S(2)}, u32[]{:S(2)}) %all-to-all-start) | async-done | bytes 458784 | tf_op jit(solution)/shard_map/all_to_all | solution.py:518
  47.2 0.8 %sum_and_spread.1 = bf16[16,112,128]{2,1,0:T(8,128)(2,1)} custom-call(bf16[16,112,128]{2,1,0:T(8,128)(2,1)S(1)} %all-to-all-done.refs_0_), custom_call_target="tpu_custom_call" | custom-call | flops 1000000 | bytes 10000 | tf_op jit(solution)/shard_map/sum_and_spread/pallas_call | solution.py:443
  48.1 3.8 %all-to-all-start.1 = ((bf16[16,112,128]{2,1,0:T(8,128)(2,1)}), bf16[16,112,128]{2,1,0:T(8,128)(2,1)S(1)}, u32[]{:S(2)}, u32[]{:S(2)}) async-start(bf16[16,112,128]{2,1,0:T(8,128)(2,1)} %sum_and_spread.1), calls=%async_computation.1 | async-start | bytes 917504 | tf_op jit(solution)/shard_map/all_to_all | solution.py:518
  51.8 11.3 %conv_run_1.1 = (bf16[3072,128]{1,0:T(8,128)(2,1)}, bf16[3072,128]{1,0:T(8,128)(2,1)}) custom-call(bf16[3072,128]{1,0:T(8,128)(2,1)} %bitcast.13, bf16[3072,128]{1,0:T(8,128)(2,1)} %bitcast.19, s32[27,24,128]{2,1,0:T(8,128)} %bitcast.26, bf16[256,3456]{1,0:T(8,128)(2,1)} %get-tuple-element.32.w_hbm, ...), custom_call_target="tpu_custom_call", output_to_operand_aliasing={{0}: (5, {}), {1}: (6, {})} | custom-call | flops 10000000000 | bytes 10000 | tf_op jit(solution)/shard_map/conv_run_1/pallas_call | solution.py:402
  63.2 2.7 %all-to-all-done.1 = bf16[16,112,128]{2,1,0:T(8,128)(2,1)S(1)} async-done(((bf16[16,112,128]{2,1,0:T(8,128)(2,1)}), bf16[16,112,128]{2,1,0:T(8,128)(2,1)S(1)}, u32[]{:S(2)}, u32[]{:S(2)}) %all-to-all-start.1) | async-done | bytes 458784 | tf_op jit(solution)/shard_map/all_to_all | solution.py:518
  65.9 0.0 collective-permute-start.3
  65.9 1.0 %widen_own_half.1.rest_0_ = f32[3456,128]{1,0:T(8,128)} custom-call(bf16[1792,128]{1,0:T(8,128)(2,1)S(1)} %bitcast.24), custom_call_target="tpu_custom_call" | custom-call | tf_op jit(solution)/shard_map/widen_own_half/pallas_call | solution.py:467
  66.8 0.9 %collective-permute-done.3.in_ref = bf16[1792,128]{1,0:T(8,128)(2,1)S(1)} collective-permute-done((bf16[1792,128]{1,0:T(8,128)(2,1)S(1)}, bf16[1792,128]{1,0:T(8,128)(2,1)S(1)}, u32[]{:S(2)}, u32[]{:S(2)}) %collective-permute-start.3) | collective-permute-done | bytes 458784 | tf_op jit(solution)/shard_map/ppermute | solution.py:529
  67.7 0.9 %widen_other_half.1 = f32[3456,128]{1,0:T(8,128)} custom-call(bf16[1792,128]{1,0:T(8,128)(2,1)S(1)} %collective-permute-done.3.in_ref, f32[3456,128]{1,0:T(8,128)} %widen_own_half.1.rest_0_), custom_call_target="tpu_custom_call", output_to_operand_aliasing={{}: (1, {})} | custom-call | tf_op jit(solution)/shard_map/widen_other_half/pallas_call | solution.py:467
  (1 shorter events, 0.0 us)
Async XLA Ops:
  0.6 6.9 %copy-start.1 = (bf16[1,3072,128]{2,1,0:T(8,128)(2,1)S(1)}, bf16[1,3072,128]{2,1,0:T(8,128)(2,1)}, u32[]{:S(2)}) copy-start(bf16[1,3072,128]{2,1,0:T(8,128)(2,1)} %param.7) | copy-start | bytes 2359300
  0.6 6.9 %copy-start = (bf16[1,3072,128]{2,1,0:T(8,128)(2,1)S(1)}, bf16[1,3072,128]{2,1,0:T(8,128)(2,1)}, u32[]{:S(2)}) copy-start(bf16[1,3072,128]{2,1,0:T(8,128)(2,1)} %param.4) | copy-start | bytes 2359300
  0.7 8.3 %copy-start.3 = (s32[1,27,3072]{2,0,1:T(1,128)S(1)}, s32[1,27,3072]{2,0,1:T(1,128)}, u32[]{:S(2)}) copy-start(s32[1,27,3072]{2,0,1:T(1,128)} %param.5) | copy-start | bytes 995332
  2.6 16.4 %collective-permute-start = (bf16[2,1024,128]{2,1,0:T(8,128)(2,1)}, bf16[2,1024,128]{2,1,0:T(8,128)(2,1)S(1)}, u32[]{:S(2)}, u32[]{:S(2)}) collective-permute-start(bf16[2,1024,128]{2,1,0:T(8,128)(2,1)} %stack_last_layer.1), channel_id=1, source_target_pairs={{0,1},{1,2},{2,3},{4,5},{5,6},{6,7},{8,9},{9,10},{10,11},{12,13},{... | collective-permute-start | bytes 1572872 | tf_op jit(solution)/shard_map/ppermute | solution.py:487
  7.6 15.3 %collective-permute-start.1 = (bf16[2,1024,128]{2,1,0:T(8,128)(2,1)S(1)}, bf16[2,1024,128]{2,1,0:T(8,128)(2,1)S(1)}, u32[]{:S(2)}, u32[]{:S(2)}) collective-permute-start(bf16[2,1024,128]{2,1,0:T(8,128)(2,1)S(1)} %stack_first_layer.1), channel_id=1, source_target_pairs={{1,0},{2,1},{3,2},{5,4},{6,5},{7,6},{9,8},{10,9},{11,10},{13,12},{... | collective-permute-start | bytes 1572872 | tf_op jit(solution)/shard_map/ppermute | solution.py:490
  19.0 2.7 %copy-start.2 = (bf16[2,1024,128]{2,1,0:T(8,128)(2,1)}, bf16[2,1024,128]{2,1,0:T(8,128)(2,1)S(1)}, u32[]{:S(2)}) copy-start(bf16[2,1024,128]{2,1,0:T(8,128)(2,1)S(1)} %collective-permute-done.low_ref.rest_0_) | copy-start | bytes 1572868
  22.9 20.7 %copy-start.4 = (bf16[2,1024,128]{2,1,0:T(8,128)(2,1)}, bf16[2,1024,128]{2,1,0:T(8,128)(2,1)S(1)}, u32[]{:S(2)}) copy-start(bf16[2,1024,128]{2,1,0:T(8,128)(2,1)S(1)} %collective-permute-done.1.rest_0_) | copy-start | bytes 1572868
  22.9 1.8 %collective-permute-start.2 = (bf16[1792,128]{1,0:T(8,128)(2,1)S(1)}, bf16[1792,128]{1,0:T(8,128)(2,1)S(1)}, u32[]{:S(2)}, u32[]{:S(2)}) collective-permute-start(bf16[1792,128]{1,0:T(8,128)(2,1)S(1)} %get-tuple-element.25), channel_id=1, source_target_pairs={{0,4},{4,0},{8,12},{12,8},{16,20},{20,16},{24,28},{28,24},{1,5},{5... | collective-permute-start | bytes 1376264 | tf_op jit(solution)/shard_map/ppermute | solution.py:504
  25.6 21.6 %all-to-all-start = ((bf16[16,112,128]{2,1,0:T(8,128)(2,1)}), bf16[16,112,128]{2,1,0:T(8,128)(2,1)S(1)}, u32[]{:S(2)}, u32[]{:S(2)}) async-start(bf16[16,112,128]{2,1,0:T(8,128)(2,1)} %bitcast.6), calls=%async_computation | async-start | bytes 917504 | tf_op jit(solution)/shard_map/all_to_all | solution.py:518
  48.1 17.8 %all-to-all-start.1 = ((bf16[16,112,128]{2,1,0:T(8,128)(2,1)}), bf16[16,112,128]{2,1,0:T(8,128)(2,1)S(1)}, u32[]{:S(2)}, u32[]{:S(2)}) async-start(bf16[16,112,128]{2,1,0:T(8,128)(2,1)} %sum_and_spread.1), calls=%async_computation.1 | async-start | bytes 917504 | tf_op jit(solution)/shard_map/all_to_all | solution.py:518
  65.9 1.8 %collective-permute-start.3 = (bf16[1792,128]{1,0:T(8,128)(2,1)S(1)}, bf16[1792,128]{1,0:T(8,128)(2,1)S(1)}, u32[]{:S(2)}, u32[]{:S(2)}) collective-permute-start(bf16[1792,128]{1,0:T(8,128)(2,1)S(1)} %bitcast.23), channel_id=1, source_target_pairs={{0,4},{4,0},{8,12},{12,8},{16,20},{20,16},{24,28},{28,24},{1,5},{5... | collective-permute-start | bytes 1376264 | tf_op jit(solution)/shard_map/ppermute | solution.py:529

commit v4 on v3

--- a/solution.py
+++ b/solution.py
@@ -451,27 +451,37 @@
     )(*parts)
 
 
-def widen_kernel(in_ref, *rest):
-    out_ref = rest[-1]
-    out_ref[...] = in_ref[...].astype(out_ref.dtype)
+def widen_kernel(own, count, in_ref, *rest):
+    out_hbm, wide, sems = rest[-3:]
+    half = in_ref.shape[0]
+    piece = half // 2
+    side = own_side() if own else 1 - own_side()
+
+    def copy(where, i):
+        first = where * half + i * piece
+        size = min(piece, count - first)
+        return pltpu.make_async_copy(
+            wide.at[pl.ds(i * piece, size), :], out_hbm.at[pl.ds(first, size), :], sems.at[i]
+        )
+
+    for i in range(2):
+        rows = slice(i * piece, (i + 1) * piece)
+        wide[rows, :] = in_ref[rows, :].astype(jnp.float32)
+        for where in range(2):
+            pl.when(side == where)(copy(where, i).start)
+    for i in range(2):
+        for where in range(2):
+            pl.when(side == where)(copy(where, i).wait)
 
 
 def widen(rows, own, count, earlier, name):
-    half, channels = rows.shape
-    block = (half // 2, channels)
-
-    def place(i):
-        side = own_side() if own else 1 - own_side()
-        return side * 2 + i, 0
-
     return pl.pallas_call(
-        widen_kernel,
-        grid=(2,),
-        in_specs=[pl.BlockSpec(block, lambda i: (i, 0))]
-        + [pl.BlockSpec(memory_space=pl.ANY)] * len(earlier),
-        out_specs=pl.BlockSpec(block, place),
-        out_shape=jax.ShapeDtypeStruct((count, channels), jnp.float32),
+        functools.partial(widen_kernel, own, count),
+        in_specs=[VMEM] + [HBM] * len(earlier),
+        out_specs=HBM,
+        out_shape=jax.ShapeDtypeStruct((count, rows.shape[1]), jnp.float32),
         input_output_aliases={1 + i: i for i in range(len(earlier))},
+        scratch_shapes=[pltpu.VMEM(rows.shape, jnp.float32), pltpu.SemaphoreType.DMA((2,))],
         compiler_params=pltpu.CompilerParams(vmem_limit_bytes=VMEM_LIMIT),
         name=name,
     )(rows, *earlier)

time: 69.1 us -> 69.2 us (level)
  no operation moved by 1% of the time
where the time goes in v4:
time: 69.2 us; the launch traced here: 68.8 us
  Pallas kernels  39.1 us (57%)
  starting transfers between devices  16.6 us (24%)
  waiting for transfers between devices  12.2 us (18%)
  between operations  0.95 us (1%)
    pallas_call x2, Pallas kernels, conv_run(): pl.pallas_call(functools.partial(conv_kernel, voxels, run, len(halos), ma...  22.8 us
    all_to_all x2, starting transfers between devices, exchange(): lax.all_to_all(pieces, ('dp', 'space'), 0, 0, axis_index_groups=alike, ti...  10.3 us
    pallas_call x1, Pallas kernels, grad_w_inner(): pl.pallas_call(functools.partial(weight_inner_kernel, voxels), out_shape=...  8.04 us
    all_to_all x2, waiting for transfers between devices, exchange(): lax.all_to_all(pieces, ('dp', 'space'), 0, 0, axis_index_groups=alike, ti...  6.32 us
    ppermute x1, starting transfers between devices, local(): lax.ppermute(stack_layer_by_copies(feats, grads, voxels // LAYER - 1, 'st...  4.96 us
    pallas_call x1, Pallas kernels, grad_w_halo(): pl.pallas_call(functools.partial(weight_halo_kernel, scale), out_shape=(o...  2.66 us
    ppermute x1, waiting for transfers between devices, local(): lax.ppermute(stack_layer_by_copies(feats, grads, voxels // LAYER - 1, 'st...  2.03 us
    pallas_call x2, Pallas kernels, widen(): pl.pallas_call(functools.partial(widen_kernel, own, count), in_specs=[VME...  1.91 us
  transfers between devices with their start and end apart: 6, of which 6 were waited for; matrix products, arithmetic and copies ran while one was open for 0% of the time, Pallas kernels for 50%

profile of v4, /device:TPU:0, one launch (start us, length us, event | category | flops | bytes accessed | tf_op | source)
XLA Modules:
  0.0 68.8 jit_solution(10681789057925008461)
XLA Ops:
  0.6 0.0 copy-start.1
  0.6 0.0 copy-start
  0.7 0.0 copy-start.3
  0.7 1.9 %stack_last_layer.1 = bf16[2,1024,128]{2,1,0:T(8,128)(2,1)} custom-call(bf16[3072,128]{1,0:T(8,128)(2,1)} %bitcast.11, bf16[3072,128]{1,0:T(8,128)(2,1)} %bitcast.17), custom_call_target="tpu_custom_call" | custom-call | tf_op jit(solution)/shard_map/stack_last_layer/pallas_call | solution.py:261
  2.6 5.0 %collective-permute-start = (bf16[2,1024,128]{2,1,0:T(8,128)(2,1)}, bf16[2,1024,128]{2,1,0:T(8,128)(2,1)S(1)}, u32[]{:S(2)}, u32[]{:S(2)}) collective-permute-start(bf16[2,1024,128]{2,1,0:T(8,128)(2,1)} %stack_last_layer.1), channel_id=1, source_target_pairs={{0,1},{1,2},{2,3},{4,5},{5,6},{6,7},{8,9},{9,10},{10,11},{12,13},{... | collective-permute-start | bytes 1572872 | tf_op jit(solution)/shard_map/ppermute | solution.py:497
  7.5 0.0 copy-done.1
  7.6 0.0 copy-done
  7.6 1.3 %collective-permute-start.1 = (bf16[2,1024,128]{2,1,0:T(8,128)(2,1)S(1)}, bf16[2,1024,128]{2,1,0:T(8,128)(2,1)S(1)}, u32[]{:S(2)}, u32[]{:S(2)}) collective-permute-start(bf16[2,1024,128]{2,1,0:T(8,128)(2,1)S(1)} %stack_first_layer.1), channel_id=1, source_target_pairs={{1,0},{2,1},{3,2},{5,4},{6,5},{7,6},{9,8},{10,9},{11,10},{13,12},{... | collective-permute-start | bytes 1572872 | tf_op jit(solution)/shard_map/ppermute | solution.py:500
  8.9 0.0 copy-done.3
  8.9 8.0 %weight_gradient_inner.1.in_ref = f32[128,3456]{1,0:T(8,128)S(1)} custom-call(bf16[3072,128]{1,0:T(8,128)(2,1)S(1)} %bitcast.15, bf16[3072,128]{1,0:T(8,128)(2,1)S(1)} %bitcast.21, s32[27,24,128]{2,1,0:T(8,128)S(1)} %bitcast.27), custom_call_target="tpu_custom_call" | custom-call | flops 8000000000 | bytes 4000000 | tf_op jit(solution)/shard_map/weight_gradient_inner/pallas_call | solution.py:189
  17.0 2.0 %collective-permute-done.low_ref.rest_0_ = bf16[2,1024,128]{2,1,0:T(8,128)(2,1)S(1)} collective-permute-done((bf16[2,1024,128]{2,1,0:T(8,128)(2,1)}, bf16[2,1024,128]{2,1,0:T(8,128)(2,1)S(1)}, u32[]{:S(2)}, u32[]{:S(2)}) %collective-permute-start) | collective-permute-done | bytes 524320 | tf_op jit(solution)/shard_map/ppermute | solution.py:497
  19.0 0.0 copy-start.2
  19.0 2.7 %weight_gradient_halo.1 = (bf16[1792,128]{1,0:T(8,128)(2,1)S(1)}, bf16[1792,128]{1,0:T(8,128)(2,1)S(1)}) custom-call(bf16[3072,128]{1,0:T(8,128)(2,1)S(1)} %bitcast.16, bf16[3072,128]{1,0:T(8,128)(2,1)S(1)} %bitcast.22, bf16[2,1024,128]{2,1,0:T(8,128)(2,1)S(1)} %collective-permute-done.low_ref.rest_0_, s32[27,24,128]{2,1,0:T(8,128)S(1)} %bitcast.28, ...), custom_call_target="tpu_custom_call" | custom-call | flops 1000000 | bytes 10000 | tf_op jit(solution)/shard_map/weight_gradient_halo/pallas_call | solution.py:204
  21.7 0.0 copy-done.2
  21.7 1.2 %collective-permute-done.1.rest_0_ = bf16[2,1024,128]{2,1,0:T(8,128)(2,1)S(1)} collective-permute-done((bf16[2,1024,128]{2,1,0:T(8,128)(2,1)S(1)}, bf16[2,1024,128]{2,1,0:T(8,128)(2,1)S(1)}, u32[]{:S(2)}, u32[]{:S(2)}) %collective-permute-start.1) | collective-permute-done | bytes 524320 | tf_op jit(solution)/shard_map/ppermute | solution.py:500
  22.9 0.0 copy-start.4
  22.9 0.0 collective-permute-start.2
  22.9 1.8 %collective-permute-done.2 = bf16[1792,128]{1,0:T(8,128)(2,1)S(1)} collective-permute-done((bf16[1792,128]{1,0:T(8,128)(2,1)S(1)}, bf16[1792,128]{1,0:T(8,128)(2,1)S(1)}, u32[]{:S(2)}, u32[]{:S(2)}) %collective-permute-start.2) | collective-permute-done | bytes 458784 | tf_op jit(solution)/shard_map/ppermute | solution.py:514
  24.7 0.9 %sum_of_pair.1 = bf16[1,1792,128]{2,1,0:T(8,128)(2,1)} custom-call(bf16[1,1792,128]{2,1,0:T(8,128)(2,1)S(1)} %bitcast.29, bf16[1,1792,128]{2,1,0:T(8,128)(2,1)S(1)} %bitcast.30), custom_call_target="tpu_custom_call" | custom-call | flops 1000000 | bytes 10000 | tf_op jit(solution)/shard_map/sum_of_pair/pallas_call | solution.py:443
  25.6 6.5 %all-to-all-start = ((bf16[16,112,128]{2,1,0:T(8,128)(2,1)}), bf16[16,112,128]{2,1,0:T(8,128)(2,1)S(1)}, u32[]{:S(2)}, u32[]{:S(2)}) async-start(bf16[16,112,128]{2,1,0:T(8,128)(2,1)} %bitcast.6), calls=%async_computation | async-start | bytes 917504 | tf_op jit(solution)/shard_map/all_to_all | solution.py:528
  32.1 11.5 %conv_run_0.1 = (bf16[3072,128]{1,0:T(8,128)(2,1)}, bf16[3072,128]{1,0:T(8,128)(2,1)}, bf16[256,3456]{1,0:T(8,128)(2,1)}) custom-call(bf16[3072,128]{1,0:T(8,128)(2,1)} %bitcast.12, bf16[3072,128]{1,0:T(8,128)(2,1)} %bitcast.18, s32[27,24,128]{2,1,0:T(8,128)} %bitcast.25, bf16[3456,128]{1,0:T(8,128)(2,1)} %bitcast.32, bf16[2,1024,128]{2,1,0:T(8,128)(2,1)} %copy-done.2), custom_call_target="tpu_custom_call" | custom-call | flops 1000000 | bytes 10000 | tf_op jit(solution)/shard_map/conv_run_0/pallas_call | solution.py:402
  43.6 0.0 copy-done.4
  43.6 3.6 %all-to-all-done.refs_0_ = bf16[16,112,128]{2,1,0:T(8,128)(2,1)S(1)} async-done(((bf16[16,112,128]{2,1,0:T(8,128)(2,1)}), bf16[16,112,128]{2,1,0:T(8,128)(2,1)S(1)}, u32[]{:S(2)}, u32[]{:S(2)}) %all-to-all-start) | async-done | bytes 458784 | tf_op jit(solution)/shard_map/all_to_all | solution.py:528
  47.2 0.8 %sum_and_spread.1 = bf16[16,112,128]{2,1,0:T(8,128)(2,1)} custom-call(bf16[16,112,128]{2,1,0:T(8,128)(2,1)S(1)} %all-to-all-done.refs_0_), custom_call_target="tpu_custom_call" | custom-call | flops 1000000 | bytes 10000 | tf_op jit(solution)/shard_map/sum_and_spread/pallas_call | solution.py:443
  48.1 3.8 %all-to-all-start.1 = ((bf16[16,112,128]{2,1,0:T(8,128)(2,1)}), bf16[16,112,128]{2,1,0:T(8,128)(2,1)S(1)}, u32[]{:S(2)}, u32[]{:S(2)}) async-start(bf16[16,112,128]{2,1,0:T(8,128)(2,1)} %sum_and_spread.1), calls=%async_computation.1 | async-start | bytes 917504 | tf_op jit(solution)/shard_map/all_to_all | solution.py:528
  51.8 11.3 %conv_run_1.1 = (bf16[3072,128]{1,0:T(8,128)(2,1)}, bf16[3072,128]{1,0:T(8,128)(2,1)}) custom-call(bf16[3072,128]{1,0:T(8,128)(2,1)} %bitcast.13, bf16[3072,128]{1,0:T(8,128)(2,1)} %bitcast.19, s32[27,24,128]{2,1,0:T(8,128)} %bitcast.26, bf16[256,3456]{1,0:T(8,128)(2,1)} %get-tuple-element.32.w_hbm, ...), custom_call_target="tpu_custom_call", output_to_operand_aliasing={{0}: (5, {}), {1}: (6, {})} | custom-call | flops 10000000000 | bytes 10000 | tf_op jit(solution)/shard_map/conv_run_1/pallas_call | solution.py:402
  63.2 2.7 %all-to-all-done.1 = bf16[16,112,128]{2,1,0:T(8,128)(2,1)S(1)} async-done(((bf16[16,112,128]{2,1,0:T(8,128)(2,1)}), bf16[16,112,128]{2,1,0:T(8,128)(2,1)S(1)}, u32[]{:S(2)}, u32[]{:S(2)}) %all-to-all-start.1) | async-done | bytes 458784 | tf_op jit(solution)/shard_map/all_to_all | solution.py:528
  65.9 0.0 collective-permute-start.3
  65.9 1.0 %widen_own_half.1.rest_0_ = f32[3456,128]{1,0:T(8,128)} custom-call(bf16[1792,128]{1,0:T(8,128)(2,1)S(1)} %bitcast.24), custom_call_target="tpu_custom_call" | custom-call | tf_op jit(solution)/shard_map/widen_own_half/pallas_call | solution.py:478
  66.9 0.8 %collective-permute-done.3.in_ref = bf16[1792,128]{1,0:T(8,128)(2,1)S(1)} collective-permute-done((bf16[1792,128]{1,0:T(8,128)(2,1)S(1)}, bf16[1792,128]{1,0:T(8,128)(2,1)S(1)}, u32[]{:S(2)}, u32[]{:S(2)}) %collective-permute-start.3) | collective-permute-done | bytes 458784 | tf_op jit(solution)/shard_map/ppermute | solution.py:539
  67.7 0.9 %widen_other_half.1 = f32[3456,128]{1,0:T(8,128)} custom-call(bf16[1792,128]{1,0:T(8,128)(2,1)S(1)} %collective-permute-done.3.in_ref, f32[3456,128]{1,0:T(8,128)} %widen_own_half.1.rest_0_), custom_call_target="tpu_custom_call", output_to_operand_aliasing={{}: (1, {})} | custom-call | tf_op jit(solution)/shard_map/widen_other_half/pallas_call | solution.py:478
  (1 shorter events, 0.0 us)
Async XLA Ops:
  0.6 6.9 %copy-start.1 = (bf16[1,3072,128]{2,1,0:T(8,128)(2,1)S(1)}, bf16[1,3072,128]{2,1,0:T(8,128)(2,1)}, u32[]{:S(2)}) copy-start(bf16[1,3072,128]{2,1,0:T(8,128)(2,1)} %param.7) | copy-start | bytes 2359300
  0.6 6.9 %copy-start = (bf16[1,3072,128]{2,1,0:T(8,128)(2,1)S(1)}, bf16[1,3072,128]{2,1,0:T(8,128)(2,1)}, u32[]{:S(2)}) copy-start(bf16[1,3072,128]{2,1,0:T(8,128)(2,1)} %param.4) | copy-start | bytes 2359300
  0.7 8.3 %copy-start.3 = (s32[1,27,3072]{2,0,1:T(1,128)S(1)}, s32[1,27,3072]{2,0,1:T(1,128)}, u32[]{:S(2)}) copy-start(s32[1,27,3072]{2,0,1:T(1,128)} %param.5) | copy-start | bytes 995332
  2.6 16.4 %collective-permute-start = (bf16[2,1024,128]{2,1,0:T(8,128)(2,1)}, bf16[2,1024,128]{2,1,0:T(8,128)(2,1)S(1)}, u32[]{:S(2)}, u32[]{:S(2)}) collective-permute-start(bf16[2,1024,128]{2,1,0:T(8,128)(2,1)} %stack_last_layer.1), channel_id=1, source_target_pairs={{0,1},{1,2},{2,3},{4,5},{5,6},{6,7},{8,9},{9,10},{10,11},{12,13},{... | collective-permute-start | bytes 1572872 | tf_op jit(solution)/shard_map/ppermute | solution.py:497
  7.6 15.3 %collective-permute-start.1 = (bf16[2,1024,128]{2,1,0:T(8,128)(2,1)S(1)}, bf16[2,1024,128]{2,1,0:T(8,128)(2,1)S(1)}, u32[]{:S(2)}, u32[]{:S(2)}) collective-permute-start(bf16[2,1024,128]{2,1,0:T(8,128)(2,1)S(1)} %stack_first_layer.1), channel_id=1, source_target_pairs={{1,0},{2,1},{3,2},{5,4},{6,5},{7,6},{9,8},{10,9},{11,10},{13,12},{... | collective-permute-start | bytes 1572872 | tf_op jit(solution)/shard_map/ppermute | solution.py:500
  19.0 2.7 %copy-start.2 = (bf16[2,1024,128]{2,1,0:T(8,128)(2,1)}, bf16[2,1024,128]{2,1,0:T(8,128)(2,1)S(1)}, u32[]{:S(2)}) copy-start(bf16[2,1024,128]{2,1,0:T(8,128)(2,1)S(1)} %collective-permute-done.low_ref.rest_0_) | copy-start | bytes 1572868
  22.9 20.7 %copy-start.4 = (bf16[2,1024,128]{2,1,0:T(8,128)(2,1)}, bf16[2,1024,128]{2,1,0:T(8,128)(2,1)S(1)}, u32[]{:S(2)}) copy-start(bf16[2,1024,128]{2,1,0:T(8,128)(2,1)S(1)} %collective-permute-done.1.rest_0_) | copy-start | bytes 1572868
  22.9 1.8 %collective-permute-start.2 = (bf16[1792,128]{1,0:T(8,128)(2,1)S(1)}, bf16[1792,128]{1,0:T(8,128)(2,1)S(1)}, u32[]{:S(2)}, u32[]{:S(2)}) collective-permute-start(bf16[1792,128]{1,0:T(8,128)(2,1)S(1)} %get-tuple-element.25), channel_id=1, source_target_pairs={{0,4},{4,0},{8,12},{12,8},{16,20},{20,16},{24,28},{28,24},{1,5},{5... | collective-permute-start | bytes 1376264 | tf_op jit(solution)/shard_map/ppermute | solution.py:514
  25.6 21.6 %all-to-all-start = ((bf16[16,112,128]{2,1,0:T(8,128)(2,1)}), bf16[16,112,128]{2,1,0:T(8,128)(2,1)S(1)}, u32[]{:S(2)}, u32[]{:S(2)}) async-start(bf16[16,112,128]{2,1,0:T(8,128)(2,1)} %bitcast.6), calls=%async_computation | async-start | bytes 917504 | tf_op jit(solution)/shard_map/all_to_all | solution.py:528
  48.1 17.8 %all-to-all-start.1 = ((bf16[16,112,128]{2,1,0:T(8,128)(2,1)}), bf16[16,112,128]{2,1,0:T(8,128)(2,1)S(1)}, u32[]{:S(2)}, u32[]{:S(2)}) async-start(bf16[16,112,128]{2,1,0:T(8,128)(2,1)} %sum_and_spread.1), calls=%async_computation.1 | async-start | bytes 917504 | tf_op jit(solution)/shard_map/all_to_all | solution.py:528
  65.9 1.8 %collective-permute-start.3 = (bf16[1792,128]{1,0:T(8,128)(2,1)S(1)}, bf16[1792,128]{1,0:T(8,128)(2,1)S(1)}, u32[]{:S(2)}, u32[]{:S(2)}) collective-permute-start(bf16[1792,128]{1,0:T(8,128)(2,1)S(1)} %bitcast.23), channel_id=1, source_target_pairs={{0,4},{4,0},{8,12},{12,8},{16,20},{20,16},{24,28},{28,24},{1,5},{5... | collective-permute-start | bytes 1376264 | tf_op jit(solution)/shard_map/ppermute | solution.py:539

commit v5 on v4

--- a/solution.py
+++ b/solution.py
@@ -1,4 +1,5 @@
 import functools
+import itertools
 import math
 
 import jax
@@ -327,11 +328,12 @@
 
     buffers = ((gf, gg), (gf2, gg2))
 
-    def product(chunk):
+    def product(chunk, sides=(0, 1)):
         rows = slice(chunk * CHUNK_C, (chunk + 1) * CHUNK_C)
         kernels = (slice(0, channels), slice(channels, 2 * channels))
         outs = ((conv_ref, conv_hbm), (gin_ref, gin_hbm))
-        for (out, out_hbm), picked, side in zip(outs, buffers[chunk % 2], kernels):
+        for i in sides:
+            (out, out_hbm), picked, side = outs[i], buffers[chunk % 2][i], kernels[i]
             total = None
             for part in range(3):
                 span = slice(part * 9 * T, (part + 1) * 9 * T)
@@ -370,9 +372,13 @@
         moves = gather_columns(
             tiles, range(27), xe, center, rel, first_tile, *buffers[chunk % 2]
         )
+        last = 0 < chunk == size // CHUNK_C - 1
+        own = [product(chunk, (0,)), product(chunk, (1,))] if last else [product(chunk)]
         for turn, _ in enumerate(moves):
-            if turn % 3 == 2:
+            if turn % (2 if last else 3) == 1 + (not last):
                 next(pending, None)
+            if last and turn in (13, 14, 16, 17):
+                next(own[(turn - 1) % 3])
             if chunk == 0 and make_wt and turn >= 4:
                 next(turning, None)
         for _ in pending:
@@ -383,7 +389,7 @@
                     pass
             else:
                 copies[-1].wait()
-        pending = product(chunk)
+        pending = itertools.chain(*own)
     for _ in pending:
         pass
     for copy in written:

time: 69.2 us -> 69.2 us (level)
  no operation moved by 1% of the time
where the time goes in v5:
time: 69.2 us; the launch traced here: 68.8 us
  Pallas kernels  39.1 us (57%)
  starting transfers between devices  16.6 us (24%)
  waiting for transfers between devices  12.1 us (17%)
  between operations  0.95 us (1%)
    pallas_call x2, Pallas kernels, conv_run(): pl.pallas_call(functools.partial(conv_kernel, voxels, run, len(halos), ma...  22.8 us
    all_to_all x2, starting transfers between devices, exchange(): lax.all_to_all(pieces, ('dp', 'space'), 0, 0, axis_index_groups=alike, ti...  10.3 us
    pallas_call x1, Pallas kernels, grad_w_inner(): pl.pallas_call(functools.partial(weight_inner_kernel, voxels), out_shape=...  8.04 us
    all_to_all x2, waiting for transfers between devices, exchange(): lax.all_to_all(pieces, ('dp', 'space'), 0, 0, axis_index_groups=alike, ti...  6.22 us
    ppermute x1, starting transfers between devices, local(): lax.ppermute(stack_layer_by_copies(feats, grads, voxels // LAYER - 1, 'st...  4.96 us
    pallas_call x1, Pallas kernels, grad_w_halo(): pl.pallas_call(functools.partial(weight_halo_kernel, scale), out_shape=(o...  2.66 us
    ppermute x1, waiting for transfers between devices, local(): lax.ppermute(stack_layer_by_copies(feats, grads, voxels // LAYER - 1, 'st...  2.03 us
    pallas_call x2, Pallas kernels, widen(): pl.pallas_call(functools.partial(widen_kernel, own, count), in_specs=[VME...  1.91 us
  transfers between devices with their start and end apart: 6, of which 6 were waited for; matrix products, arithmetic and copies ran while one was open for 0% of the time, Pallas kernels for 50%

profile of v5, /device:TPU:0, one launch (start us, length us, event | category | flops | bytes accessed | tf_op | source)
XLA Modules:
  0.0 68.8 jit_solution(15421006849431624538)
XLA Ops:
  0.6 0.0 copy-start.1
  0.6 0.0 copy-start
  0.7 0.0 copy-start.3
  0.7 1.9 %stack_last_layer.1 = bf16[2,1024,128]{2,1,0:T(8,128)(2,1)} custom-call(bf16[3072,128]{1,0:T(8,128)(2,1)} %bitcast.11, bf16[3072,128]{1,0:T(8,128)(2,1)} %bitcast.17), custom_call_target="tpu_custom_call" | custom-call | tf_op jit(solution)/shard_map/stack_last_layer/pallas_call | solution.py:262
  2.6 5.0 %collective-permute-start = (bf16[2,1024,128]{2,1,0:T(8,128)(2,1)}, bf16[2,1024,128]{2,1,0:T(8,128)(2,1)S(1)}, u32[]{:S(2)}, u32[]{:S(2)}) collective-permute-start(bf16[2,1024,128]{2,1,0:T(8,128)(2,1)} %stack_last_layer.1), channel_id=1, source_target_pairs={{0,1},{1,2},{2,3},{4,5},{5,6},{6,7},{8,9},{9,10},{10,11},{12,13},{... | collective-permute-start | bytes 1572872 | tf_op jit(solution)/shard_map/ppermute | solution.py:503
  7.5 0.0 copy-done.1
  7.6 0.0 copy-done
  7.6 1.3 %collective-permute-start.1 = (bf16[2,1024,128]{2,1,0:T(8,128)(2,1)S(1)}, bf16[2,1024,128]{2,1,0:T(8,128)(2,1)S(1)}, u32[]{:S(2)}, u32[]{:S(2)}) collective-permute-start(bf16[2,1024,128]{2,1,0:T(8,128)(2,1)S(1)} %stack_first_layer.1), channel_id=1, source_target_pairs={{1,0},{2,1},{3,2},{5,4},{6,5},{7,6},{9,8},{10,9},{11,10},{13,12},{... | collective-permute-start | bytes 1572872 | tf_op jit(solution)/shard_map/ppermute | solution.py:506
  8.9 0.0 copy-done.3
  8.9 8.0 %weight_gradient_inner.1.in_ref = f32[128,3456]{1,0:T(8,128)S(1)} custom-call(bf16[3072,128]{1,0:T(8,128)(2,1)S(1)} %bitcast.15, bf16[3072,128]{1,0:T(8,128)(2,1)S(1)} %bitcast.21, s32[27,24,128]{2,1,0:T(8,128)S(1)} %bitcast.27), custom_call_target="tpu_custom_call" | custom-call | flops 8000000000 | bytes 4000000 | tf_op jit(solution)/shard_map/weight_gradient_inner/pallas_call | solution.py:190
  17.0 2.0 %collective-permute-done.low_ref.rest_0_ = bf16[2,1024,128]{2,1,0:T(8,128)(2,1)S(1)} collective-permute-done((bf16[2,1024,128]{2,1,0:T(8,128)(2,1)}, bf16[2,1024,128]{2,1,0:T(8,128)(2,1)S(1)}, u32[]{:S(2)}, u32[]{:S(2)}) %collective-permute-start) | collective-permute-done | bytes 524320 | tf_op jit(solution)/shard_map/ppermute | solution.py:503
  19.0 0.0 copy-start.2
  19.0 2.7 %weight_gradient_halo.1 = (bf16[1792,128]{1,0:T(8,128)(2,1)S(1)}, bf16[1792,128]{1,0:T(8,128)(2,1)S(1)}) custom-call(bf16[3072,128]{1,0:T(8,128)(2,1)S(1)} %bitcast.16, bf16[3072,128]{1,0:T(8,128)(2,1)S(1)} %bitcast.22, bf16[2,1024,128]{2,1,0:T(8,128)(2,1)S(1)} %collective-permute-done.low_ref.rest_0_, s32[27,24,128]{2,1,0:T(8,128)S(1)} %bitcast.28, ...), custom_call_target="tpu_custom_call" | custom-call | flops 1000000 | bytes 10000 | tf_op jit(solution)/shard_map/weight_gradient_halo/pallas_call | solution.py:205
  21.7 0.0 copy-done.2
  21.7 1.2 %collective-permute-done.1.rest_0_ = bf16[2,1024,128]{2,1,0:T(8,128)(2,1)S(1)} collective-permute-done((bf16[2,1024,128]{2,1,0:T(8,128)(2,1)S(1)}, bf16[2,1024,128]{2,1,0:T(8,128)(2,1)S(1)}, u32[]{:S(2)}, u32[]{:S(2)}) %collective-permute-start.1) | collective-permute-done | bytes 524320 | tf_op jit(solution)/shard_map/ppermute | solution.py:506
  22.9 0.0 copy-start.4
  22.9 0.0 collective-permute-start.2
  22.9 1.8 %collective-permute-done.2 = bf16[1792,128]{1,0:T(8,128)(2,1)S(1)} collective-permute-done((bf16[1792,128]{1,0:T(8,128)(2,1)S(1)}, bf16[1792,128]{1,0:T(8,128)(2,1)S(1)}, u32[]{:S(2)}, u32[]{:S(2)}) %collective-permute-start.2) | collective-permute-done | bytes 458784 | tf_op jit(solution)/shard_map/ppermute | solution.py:520
  24.7 0.9 %sum_of_pair.1 = bf16[1,1792,128]{2,1,0:T(8,128)(2,1)} custom-call(bf16[1,1792,128]{2,1,0:T(8,128)(2,1)S(1)} %bitcast.29, bf16[1,1792,128]{2,1,0:T(8,128)(2,1)S(1)} %bitcast.30), custom_call_target="tpu_custom_call" | custom-call | flops 1000000 | bytes 10000 | tf_op jit(solution)/shard_map/sum_of_pair/pallas_call | solution.py:449
  25.6 6.5 %all-to-all-start = ((bf16[16,112,128]{2,1,0:T(8,128)(2,1)}), bf16[16,112,128]{2,1,0:T(8,128)(2,1)S(1)}, u32[]{:S(2)}, u32[]{:S(2)}) async-start(bf16[16,112,128]{2,1,0:T(8,128)(2,1)} %bitcast.6), calls=%async_computation | async-start | bytes 917504 | tf_op jit(solution)/shard_map/all_to_all | solution.py:534
  32.1 11.4 %conv_run_0.1 = (bf16[3072,128]{1,0:T(8,128)(2,1)}, bf16[3072,128]{1,0:T(8,128)(2,1)}, bf16[256,3456]{1,0:T(8,128)(2,1)}) custom-call(bf16[3072,128]{1,0:T(8,128)(2,1)} %bitcast.12, bf16[3072,128]{1,0:T(8,128)(2,1)} %bitcast.18, s32[27,24,128]{2,1,0:T(8,128)} %bitcast.25, bf16[3456,128]{1,0:T(8,128)(2,1)} %bitcast.32, bf16[2,1024,128]{2,1,0:T(8,128)(2,1)} %copy-done.2), custom_call_target="tpu_custom_call" | custom-call | flops 1000000 | bytes 10000 | tf_op jit(solution)/shard_map/conv_run_0/pallas_call | solution.py:408
  43.5 0.0 copy-done.4
  43.5 3.7 %all-to-all-done.refs_0_ = bf16[16,112,128]{2,1,0:T(8,128)(2,1)S(1)} async-done(((bf16[16,112,128]{2,1,0:T(8,128)(2,1)}), bf16[16,112,128]{2,1,0:T(8,128)(2,1)S(1)}, u32[]{:S(2)}, u32[]{:S(2)}) %all-to-all-start) | async-done | bytes 458784 | tf_op jit(solution)/shard_map/all_to_all | solution.py:534
  47.2 0.8 %sum_and_spread.1 = bf16[16,112,128]{2,1,0:T(8,128)(2,1)} custom-call(bf16[16,112,128]{2,1,0:T(8,128)(2,1)S(1)} %all-to-all-done.refs_0_), custom_call_target="tpu_custom_call" | custom-call | flops 1000000 | bytes 10000 | tf_op jit(solution)/shard_map/sum_and_spread/pallas_call | solution.py:449
  48.1 3.8 %all-to-all-start.1 = ((bf16[16,112,128]{2,1,0:T(8,128)(2,1)}), bf16[16,112,128]{2,1,0:T(8,128)(2,1)S(1)}, u32[]{:S(2)}, u32[]{:S(2)}) async-start(bf16[16,112,128]{2,1,0:T(8,128)(2,1)} %sum_and_spread.1), calls=%async_computation.1 | async-start | bytes 917504 | tf_op jit(solution)/shard_map/all_to_all | solution.py:534
  51.8 11.4 %conv_run_1.1 = (bf16[3072,128]{1,0:T(8,128)(2,1)}, bf16[3072,128]{1,0:T(8,128)(2,1)}) custom-call(bf16[3072,128]{1,0:T(8,128)(2,1)} %bitcast.13, bf16[3072,128]{1,0:T(8,128)(2,1)} %bitcast.19, s32[27,24,128]{2,1,0:T(8,128)} %bitcast.26, bf16[256,3456]{1,0:T(8,128)(2,1)} %get-tuple-element.32.w_hbm, ...), custom_call_target="tpu_custom_call", output_to_operand_aliasing={{0}: (5, {}), {1}: (6, {})} | custom-call | flops 10000000000 | bytes 10000 | tf_op jit(solution)/shard_map/conv_run_1/pallas_call | solution.py:408
  63.3 2.5 %all-to-all-done.1 = bf16[16,112,128]{2,1,0:T(8,128)(2,1)S(1)} async-done(((bf16[16,112,128]{2,1,0:T(8,128)(2,1)}), bf16[16,112,128]{2,1,0:T(8,128)(2,1)S(1)}, u32[]{:S(2)}, u32[]{:S(2)}) %all-to-all-start.1) | async-done | bytes 458784 | tf_op jit(solution)/shard_map/all_to_all | solution.py:534
  65.8 0.0 collective-permute-start.3
  65.8 1.0 %widen_own_half.1.rest_0_ = f32[3456,128]{1,0:T(8,128)} custom-call(bf16[1792,128]{1,0:T(8,128)(2,1)S(1)} %bitcast.24), custom_call_target="tpu_custom_call" | custom-call | tf_op jit(solution)/shard_map/widen_own_half/pallas_call | solution.py:484
  66.8 0.8 %collective-permute-done.3.in_ref = bf16[1792,128]{1,0:T(8,128)(2,1)S(1)} collective-permute-done((bf16[1792,128]{1,0:T(8,128)(2,1)S(1)}, bf16[1792,128]{1,0:T(8,128)(2,1)S(1)}, u32[]{:S(2)}, u32[]{:S(2)}) %collective-permute-start.3) | collective-permute-done | bytes 458784 | tf_op jit(solution)/shard_map/ppermute | solution.py:545
  67.6 0.9 %widen_other_half.1 = f32[3456,128]{1,0:T(8,128)} custom-call(bf16[1792,128]{1,0:T(8,128)(2,1)S(1)} %collective-permute-done.3.in_ref, f32[3456,128]{1,0:T(8,128)} %widen_own_half.1.rest_0_), custom_call_target="tpu_custom_call", output_to_operand_aliasing={{}: (1, {})} | custom-call | tf_op jit(solution)/shard_map/widen_other_half/pallas_call | solution.py:484
  (1 shorter events, 0.0 us)
Async XLA Ops:
  0.6 6.9 %copy-start.1 = (bf16[1,3072,128]{2,1,0:T(8,128)(2,1)S(1)}, bf16[1,3072,128]{2,1,0:T(8,128)(2,1)}, u32[]{:S(2)}) copy-start(bf16[1,3072,128]{2,1,0:T(8,128)(2,1)} %param.7) | copy-start | bytes 2359300
  0.6 6.9 %copy-start = (bf16[1,3072,128]{2,1,0:T(8,128)(2,1)S(1)}, bf16[1,3072,128]{2,1,0:T(8,128)(2,1)}, u32[]{:S(2)}) copy-start(bf16[1,3072,128]{2,1,0:T(8,128)(2,1)} %param.4) | copy-start | bytes 2359300
  0.7 8.3 %copy-start.3 = (s32[1,27,3072]{2,0,1:T(1,128)S(1)}, s32[1,27,3072]{2,0,1:T(1,128)}, u32[]{:S(2)}) copy-start(s32[1,27,3072]{2,0,1:T(1,128)} %param.5) | copy-start | bytes 995332
  2.6 16.4 %collective-permute-start = (bf16[2,1024,128]{2,1,0:T(8,128)(2,1)}, bf16[2,1024,128]{2,1,0:T(8,128)(2,1)S(1)}, u32[]{:S(2)}, u32[]{:S(2)}) collective-permute-start(bf16[2,1024,128]{2,1,0:T(8,128)(2,1)} %stack_last_layer.1), channel_id=1, source_target_pairs={{0,1},{1,2},{2,3},{4,5},{5,6},{6,7},{8,9},{9,10},{10,11},{12,13},{... | collective-permute-start | bytes 1572872 | tf_op jit(solution)/shard_map/ppermute | solution.py:503
  7.6 15.3 %collective-permute-start.1 = (bf16[2,1024,128]{2,1,0:T(8,128)(2,1)S(1)}, bf16[2,1024,128]{2,1,0:T(8,128)(2,1)S(1)}, u32[]{:S(2)}, u32[]{:S(2)}) collective-permute-start(bf16[2,1024,128]{2,1,0:T(8,128)(2,1)S(1)} %stack_first_layer.1), channel_id=1, source_target_pairs={{1,0},{2,1},{3,2},{5,4},{6,5},{7,6},{9,8},{10,9},{11,10},{13,12},{... | collective-permute-start | bytes 1572872 | tf_op jit(solution)/shard_map/ppermute | solution.py:506
  19.0 2.7 %copy-start.2 = (bf16[2,1024,128]{2,1,0:T(8,128)(2,1)}, bf16[2,1024,128]{2,1,0:T(8,128)(2,1)S(1)}, u32[]{:S(2)}) copy-start(bf16[2,1024,128]{2,1,0:T(8,128)(2,1)S(1)} %collective-permute-done.low_ref.rest_0_) | copy-start | bytes 1572868
  22.9 20.6 %copy-start.4 = (bf16[2,1024,128]{2,1,0:T(8,128)(2,1)}, bf16[2,1024,128]{2,1,0:T(8,128)(2,1)S(1)}, u32[]{:S(2)}) copy-start(bf16[2,1024,128]{2,1,0:T(8,128)(2,1)S(1)} %collective-permute-done.1.rest_0_) | copy-start | bytes 1572868
  22.9 1.8 %collective-permute-start.2 = (bf16[1792,128]{1,0:T(8,128)(2,1)S(1)}, bf16[1792,128]{1,0:T(8,128)(2,1)S(1)}, u32[]{:S(2)}, u32[]{:S(2)}) collective-permute-start(bf16[1792,128]{1,0:T(8,128)(2,1)S(1)} %get-tuple-element.25), channel_id=1, source_target_pairs={{0,4},{4,0},{8,12},{12,8},{16,20},{20,16},{24,28},{28,24},{1,5},{5... | collective-permute-start | bytes 1376264 | tf_op jit(solution)/shard_map/ppermute | solution.py:520
  25.6 21.6 %all-to-all-start = ((bf16[16,112,128]{2,1,0:T(8,128)(2,1)}), bf16[16,112,128]{2,1,0:T(8,128)(2,1)S(1)}, u32[]{:S(2)}, u32[]{:S(2)}) async-start(bf16[16,112,128]{2,1,0:T(8,128)(2,1)} %bitcast.6), calls=%async_computation | async-start | bytes 917504 | tf_op jit(solution)/shard_map/all_to_all | solution.py:534
  48.1 17.8 %all-to-all-start.1 = ((bf16[16,112,128]{2,1,0:T(8,128)(2,1)}), bf16[16,112,128]{2,1,0:T(8,128)(2,1)S(1)}, u32[]{:S(2)}, u32[]{:S(2)}) async-start(bf16[16,112,128]{2,1,0:T(8,128)(2,1)} %sum_and_spread.1), calls=%async_computation.1 | async-start | bytes 917504 | tf_op jit(solution)/shard_map/all_to_all | solution.py:534
  65.8 1.8 %collective-permute-start.3 = (bf16[1792,128]{1,0:T(8,128)(2,1)S(1)}, bf16[1792,128]{1,0:T(8,128)(2,1)S(1)}, u32[]{:S(2)}, u32[]{:S(2)}) collective-permute-start(bf16[1792,128]{1,0:T(8,128)(2,1)S(1)} %bitcast.23), channel_id=1, source_target_pairs={{0,4},{4,0},{8,12},{12,8},{16,20},{20,16},{24,28},{28,24},{1,5},{5... | collective-permute-start | bytes 1376264 | tf_op jit(solution)/shard_map/ppermute | solution.py:545
